TPU v7x, 32 devices: a whole 2x2x4 slice. The times are simulated.
32 devices in a mesh: rad: 8 (over y, x, core), azi: 4 (over z).
Axes of the slice: x: 2, y: 2, z: 4, core: 2. Of those that a mesh axis runs over, the one named last changes fastest.
Arguments:
- fields: float32 [5, 256, 64, 128], P(None, 'rad', 'azi'), may hold values from -6 to 6
- kappa: float32 [256, 64, 128], P('rad', 'azi'), may hold values from 0.01 to 0.1
- radial_speed: float32 [5, 256], P(None, 'rad'), may hold values from -0.5 to 0.5
- azimuth_speed: float32 [5, 256], P(None, 'rad'), may hold values from -0.5 to 0.5
- shifts: int32 [256], P('rad'), may hold values from 0 to 63
Outputs:
- advanced: float32 [5, 256, 64, 128], P(None, 'rad', 'azi')
All inputs are finite; a program needn't handle non-finite values.
Results may differ from a plain program's by a relative error of at most 0.00002.
Values sent between devices are 32-bit elements; how exact they have to be, the bound alone decides.
A program may use at most 64 MiB of HBM per device.

v0:
```python
import jax
import jax.numpy as jnp
from jax import lax
from jax.sharding import PartitionSpec as P


def with_halo(cells, sides, width, closed):
    for axis, dim in sides:
        count = lax.axis_size(axis)
        ends = count if closed else count - 1
        head = lax.slice_in_dim(cells, 0, width, axis=dim)
        tail = lax.slice_in_dim(cells, cells.shape[dim] - width, cells.shape[dim], axis=dim)
        cells = jnp.concatenate(
            [
                lax.ppermute(tail, axis, [(i, (i + 1) % count) for i in range(ends)]),
                cells,
                lax.ppermute(head, axis, [((i + 1) % count, i) for i in range(ends)]),
            ],
            axis=dim,
        )
    return cells


def stencil(padded, kap, speed_r, speed_p):
    n_r = padded.shape[1] - 4
    n_p = padded.shape[2] - 4

    def tap(a, b):
        return padded[:, 2 + a : 2 + a + n_r, 2 + b : 2 + b + n_p, :]

    centre = tap(0, 0)
    height = centre.shape[3]
    zpad = jnp.pad(centre, ((0, 0), (0, 0), (0, 0), (2, 2)))

    def ztap(a):
        return zpad[:, :, :, 2 + a : 2 + a + height]

    first_r = (tap(-2, 0) - 8.0 * tap(-1, 0) + 8.0 * tap(1, 0) - tap(2, 0)) / 12.0
    first_p = (tap(0, -2) - 8.0 * tap(0, -1) + 8.0 * tap(0, 1) - tap(0, 2)) / 12.0
    second_r = (
        -tap(-2, 0) + 16.0 * tap(-1, 0) - 30.0 * centre + 16.0 * tap(1, 0) - tap(2, 0)
    ) / 12.0
    second_p = (
        -tap(0, -2) + 16.0 * tap(0, -1) - 30.0 * centre + 16.0 * tap(0, 1) - tap(0, 2)
    ) / 12.0
    second_z = (-ztap(-2) + 16.0 * ztap(-1) - 30.0 * centre + 16.0 * ztap(1) - ztap(2)) / 12.0
    return (
        -speed_r[:, :, None, None] * first_r
        - speed_p[:, :, None, None] * first_p
        + kap[None] * (second_r + second_p + second_z)
    )


def extend(field, width):
    beside_all = with_halo(field, (("azi", 2),), width, True)
    return with_halo(beside_all, (("rad", 1),), width, False)


def heun_sections(field, kappa, speed_r, speed_p):
    first = field + stencil(extend(field, 2), kappa, speed_r, speed_p)
    return 0.5 * (field + first + stencil(extend(first, 2), kappa, speed_r, speed_p))


def rotate_rows(joined, offset, length):
    current = joined
    for level in range((length - 1).bit_length()):
        step_size = 1 << level
        pushed = jnp.concatenate(
            [jnp.zeros_like(current[:, :, :step_size]), current[:, :, :-step_size]], axis=2
        )
        chosen = offset // step_size % 2 == 1
        current = jnp.where(chosen[None, :, None, None], pushed, current)
    return current[:, :, length : 2 * length]


def shift_rows(half, shifts):
    turned = lax.all_to_all(half, "azi", split_axis=1, concat_axis=2, tiled=True)
    mine = turned.shape[1]
    count = turned.shape[2]
    own = lax.dynamic_slice_in_dim(shifts, lax.axis_index("azi") * mine, mine)
    joined = jnp.concatenate([turned, turned], axis=2)
    rolled = rotate_rows(joined, own, count)
    return lax.all_to_all(rolled, "azi", split_axis=2, concat_axis=1, tiled=True)


def shards(fields, kappa, radial_speed, azimuth_speed, shifts):
    half = heun_sections(fields, kappa, radial_speed, azimuth_speed)
    moved = shift_rows(half, shifts)
    return heun_sections(moved, kappa, radial_speed, azimuth_speed)


def solution(mesh):
    placed = (
        P(None, "rad", "azi", None),
        P("rad", "azi", None),
        P(None, "rad"),
        P(None, "rad"),
        P("rad"),
    )
    return jax.shard_map(
        shards, mesh=mesh, in_specs=placed, out_specs=P(None, "rad", "azi", None), check_vma=False
    )
```

profile of v0, /device:TPU:1, one launch (start us, length us, event | category | flops | bytes accessed | tf_op | source)
XLA Modules:
  0.0 173.7 jit_solution(2678266426569322432)
XLA Ops:
  0.0 1.4 fusion.73
  1.4 2.2 %collective-permute-start = (f32[5,32,2,128]{3,2,1,0:T(2,128)S(1)}, f32[5,32,2,128]{3,2,1,0:T(2,128)S(1)}, u32[]{:S(2)}, u32[]{:S(2)}) collective-permute-start(f32[5,32,2,128]{3,2,1,0:T(2,128)S(1)} %get-tuple-element.31), channel_id=1, source_target_pairs={{0,1},{1,2},{2,3},{3,0},{4,5},{5,6},{6,7},{7,4},{8,9},{9,10},{10,1... | collective-permute-start | bytes 491528 | tf_op jit(solution)/shard_map/ppermute | solution.py:15
  3.6 2.1 %collective-permute-start.1 = (f32[5,32,2,128]{3,2,1,0:T(2,128)S(1)}, f32[5,32,2,128]{3,2,1,0:T(2,128)S(1)}, u32[]{:S(2)}, u32[]{:S(2)}) collective-permute-start(f32[5,32,2,128]{3,2,1,0:T(2,128)S(1)} %get-tuple-element.32), channel_id=1, source_target_pairs={{1,0},{2,1},{3,2},{0,3},{5,4},{6,5},{7,6},{4,7},{9,8},{10,9},{11,1... | collective-permute-start | bytes 491528 | tf_op jit(solution)/shard_map/ppermute | solution.py:17
  5.7 1.0 broadcast_multiply_fusion
  6.7 0.7 negate_multiply_fusion
  7.4 1.5 constant_dynamic-update-slice_fusion.1
  8.9 0.7 collective-permute-done
  9.6 3.0 %collective-permute-done.1 = f32[5,32,2,128]{3,2,1,0:T(2,128)S(1)} collective-permute-done((f32[5,32,2,128]{3,2,1,0:T(2,128)S(1)}, f32[5,32,2,128]{3,2,1,0:T(2,128)S(1)}, u32[]{:S(2)}, u32[]{:S(2)}) %collective-permute-start.1) | collective-permute-done | bytes 163872 | tf_op jit(solution)/shard_map/ppermute | solution.py:17
  12.6 4.1 %collective-permute-start.2 = (f32[5,2,20,128]{3,2,1,0:T(8,128)S(1)}, f32[5,2,20,128]{3,2,1,0:T(8,128)S(1)}, u32[]{:S(2)}, u32[]{:S(2)}) collective-permute-start(f32[5,2,20,128]{3,2,1,0:T(8,128)S(1)} %get-tuple-element.23), channel_id=1, source_target_pairs={{0,4},{4,8},{8,12},{12,16},{16,20},{20,24},{24,28},{1,5},{5,9},{9,... | collective-permute-start | bytes 307208 | tf_op jit(solution)/shard_map/ppermute | solution.py:15
  16.8 1.9 %collective-permute-start.3 = (f32[5,2,20,128]{3,2,1,0:T(8,128)S(1)}, f32[5,2,20,128]{3,2,1,0:T(8,128)S(1)}, u32[]{:S(2)}, u32[]{:S(2)}) collective-permute-start(f32[5,2,20,128]{3,2,1,0:T(8,128)S(1)} %get-tuple-element.24), channel_id=1, source_target_pairs={{4,0},{8,4},{12,8},{16,12},{20,16},{24,20},{28,24},{5,1},{9,5},{13... | collective-permute-start | bytes 307208 | tf_op jit(solution)/shard_map/ppermute | solution.py:17
  18.8 4.2 %collective-permute-done.3 = f32[5,2,20,128]{3,2,1,0:T(8,128)S(1)} collective-permute-done((f32[5,2,20,128]{3,2,1,0:T(8,128)S(1)}, f32[5,2,20,128]{3,2,1,0:T(8,128)S(1)}, u32[]{:S(2)}, u32[]{:S(2)}) %collective-permute-start.3) | collective-permute-done | bytes 102432 | tf_op jit(solution)/shard_map/ppermute | solution.py:17
  23.0 0.4 maximum_maximum_fusion
  23.3 3.6 %fusion.17 = f32[5,32,16,128]{3,2,1,0:T(8,128)S(1)} fusion(f32[5,32,16,128]{3,2,1,0:T(8,128)S(1)} %copy-done, f32[5,32,18,128]{3,2,1,0:T(8,128)S(1)} %constant_dynamic-update-slice_fusion, f32[5,32,2,128]{3,2,1,0:T(2,128)S(1)} %collective-permute-done, f32[5,34,20,128]{3,2,1,0:T(8,128)S(1)} %get-tuple-element.22, ...), kind=kLoop, calls=%fused_computation.62 | loop fusion | flops 13762560 | bytes 10913024 | tf_op jit(solution)/shard_map/add | solution.py:60
  27.1 0.9 collective-permute-start.4
  28.0 2.4 %collective-permute-start.5 = (f32[5,32,2,128]{3,2,1,0:T(2,128)S(1)}, f32[5,32,2,128]{3,2,1,0:T(2,128)S(1)}, u32[]{:S(2)}, u32[]{:S(2)}) collective-permute-start(f32[5,32,2,128]{3,2,1,0:T(2,128)S(1)} %get-tuple-element.30), channel_id=1, source_target_pairs={{1,0},{2,1},{3,2},{0,3},{5,4},{6,5},{7,6},{4,7},{9,8},{10,9},{11,1... | collective-permute-start | bytes 491528 | tf_op jit(solution)/shard_map/ppermute | solution.py:17
  30.4 3.9 %collective-permute-done.4 = f32[5,32,2,128]{3,2,1,0:T(2,128)S(1)} collective-permute-done((f32[5,32,2,128]{3,2,1,0:T(2,128)S(1)}, f32[5,32,2,128]{3,2,1,0:T(2,128)S(1)}, u32[]{:S(2)}, u32[]{:S(2)}) %collective-permute-start.4) | collective-permute-done | bytes 163872 | tf_op jit(solution)/shard_map/ppermute | solution.py:15
  34.4 0.9 collective-permute-done.5
  35.3 4.6 %collective-permute-start.6 = (f32[5,2,20,128]{3,2,1,0:T(8,128)S(1)}, f32[5,2,20,128]{3,2,1,0:T(8,128)S(1)}, u32[]{:S(2)}, u32[]{:S(2)}) collective-permute-start(f32[5,2,20,128]{3,2,1,0:T(8,128)S(1)} %get-tuple-element.19), channel_id=1, source_target_pairs={{0,4},{4,8},{8,12},{12,16},{16,20},{20,24},{24,28},{1,5},{5,9},{9,... | collective-permute-start | bytes 307208 | tf_op jit(solution)/shard_map/ppermute | solution.py:15
  39.9 1.9 %collective-permute-start.7 = (f32[5,2,20,128]{3,2,1,0:T(8,128)S(1)}, f32[5,2,20,128]{3,2,1,0:T(8,128)S(1)}, u32[]{:S(2)}, u32[]{:S(2)}) collective-permute-start(f32[5,2,20,128]{3,2,1,0:T(8,128)S(1)} %get-tuple-element.20), channel_id=1, source_target_pairs={{4,0},{8,4},{12,8},{16,12},{20,16},{24,20},{28,24},{5,1},{9,5},{13... | collective-permute-start | bytes 307208 | tf_op jit(solution)/shard_map/ppermute | solution.py:17
  41.8 4.3 %collective-permute-done.7 = f32[5,2,20,128]{3,2,1,0:T(8,128)S(1)} collective-permute-done((f32[5,2,20,128]{3,2,1,0:T(8,128)S(1)}, f32[5,2,20,128]{3,2,1,0:T(8,128)S(1)}, u32[]{:S(2)}, u32[]{:S(2)}) %collective-permute-start.7) | collective-permute-done | bytes 102432 | tf_op jit(solution)/shard_map/ppermute | solution.py:17
  46.1 0.4 maximum_maximum_fusion.1
  46.4 3.8 %fusion.29 = f32[5,32,16,128]{3,2,1,0:T(8,128)S(1)} fusion(f32[5,32,16,128]{3,2,1,0:T(8,128)S(1)} %fusion.17, f32[5,32,2,128]{3,2,1,0:T(2,128)S(1)} %collective-permute-done.5, f32[5,32,2,128]{3,2,1,0:T(2,128)S(1)} %collective-permute-done.4, f32[5,34,20,128]{3,2,1,0:T(8,128)S(1)} %get-tuple-element.18, f32[5,34,20,128]{3,2,1,0:T(8,128)S(1)} %get-tuple-element.17, ...), kind=kLoop, calls=%fused_computation.74 | loop fusion | flops 15073280 | bytes 9766144 | tf_op jit(solution)/shard_map/mul | solution.py:61
  50.2 1.1 copy.8
  51.4 3.7 %all-to-all-start = ((f32[5,32,16,128]{3,2,0,1:T(8,128)}), f32[5,32,16,128]{3,2,0,1:T(8,128)S(1)}, u32[]{:S(2)}, u32[]{:S(2)}) async-start(f32[5,32,16,128]{3,2,0,1:T(8,128)} %copy.8), calls=%async_computation | async-start | bytes 2621440 | tf_op jit(solution)/shard_map/all_to_all | solution.py:77
  55.2 28.9 %all-to-all-done = f32[5,32,16,128]{3,2,0,1:T(8,128)S(1)} async-done(((f32[5,32,16,128]{3,2,0,1:T(8,128)}), f32[5,32,16,128]{3,2,0,1:T(8,128)S(1)}, u32[]{:S(2)}, u32[]{:S(2)}) %all-to-all-start) | async-done | bytes 1310752 | tf_op jit(solution)/shard_map/all_to_all | solution.py:77
  84.6 0.8 fusion.1
  85.4 0.8 pad_select_fusion.3
  86.2 0.6 pad_select_fusion.2
  87.1 0.5 pad_select_fusion.1
  87.8 0.4 pad_select_fusion
  88.6 0.8 copy.11
  89.3 34.3 %all_to_all.36 = f32[5,8,64,128]{3,1,0,2:T(8,128)S(1)} all-to-all(f32[5,8,64,128]{3,1,0,2:T(8,128)S(1)} %copy.11), channel_id=1, replica_groups=mesh['rad'=8,'azi'=4] {'azi'}, dimensions={2} | all-to-all | bytes 2621440 | tf_op jit(solution)/shard_map/all_to_all | solution.py:83
  124.1 3.3 %collective-permute-start.9 = (f32[5,32,2,128]{3,2,1,0:T(2,128)S(1)}, f32[5,32,2,128]{3,2,1,0:T(2,128)S(1)}, u32[]{:S(2)}, u32[]{:S(2)}) collective-permute-start(f32[5,32,2,128]{3,2,1,0:T(2,128)S(1)} %get-tuple-element.28), channel_id=1, source_target_pairs={{1,0},{2,1},{3,2},{0,3},{5,4},{6,5},{7,6},{4,7},{9,8},{10,9},{11,1... | collective-permute-start | bytes 491528 | tf_op jit(solution)/shard_map/ppermute | solution.py:17
  127.4 3.9 %collective-permute-done.8 = f32[5,32,2,128]{3,2,1,0:T(2,128)S(1)} collective-permute-done((f32[5,32,2,128]{3,2,1,0:T(2,128)S(1)}, f32[5,32,2,128]{3,2,1,0:T(2,128)S(1)}, u32[]{:S(2)}, u32[]{:S(2)}) %collective-permute-start.8) | collective-permute-done | bytes 163872 | tf_op jit(solution)/shard_map/ppermute | solution.py:15
  131.2 1.6 collective-permute-done.9
  132.9 6.2 %collective-permute-start.10 = (f32[5,2,20,128]{3,2,1,0:T(8,128)S(1)}, f32[5,2,20,128]{3,2,1,0:T(8,128)S(1)}, u32[]{:S(2)}, u32[]{:S(2)}) collective-permute-start(f32[5,2,20,128]{3,2,1,0:T(8,128)S(1)} %get-tuple-element.15), channel_id=1, source_target_pairs={{0,4},{4,8},{8,12},{12,16},{16,20},{20,24},{24,28},{1,5},{5,9},{9,... | collective-permute-start | bytes 307208 | tf_op jit(solution)/shard_map/ppermute | solution.py:15
  139.1 1.9 %collective-permute-start.11 = (f32[5,2,20,128]{3,2,1,0:T(8,128)S(1)}, f32[5,2,20,128]{3,2,1,0:T(8,128)S(1)}, u32[]{:S(2)}, u32[]{:S(2)}) collective-permute-start(f32[5,2,20,128]{3,2,1,0:T(8,128)S(1)} %get-tuple-element.16), channel_id=1, source_target_pairs={{4,0},{8,4},{12,8},{16,12},{20,16},{24,20},{28,24},{5,1},{9,5},{13... | collective-permute-start | bytes 307208 | tf_op jit(solution)/shard_map/ppermute | solution.py:17
  141.0 4.3 %collective-permute-done.11 = f32[5,2,20,128]{3,2,1,0:T(8,128)S(1)} collective-permute-done((f32[5,2,20,128]{3,2,1,0:T(8,128)S(1)}, f32[5,2,20,128]{3,2,1,0:T(8,128)S(1)}, u32[]{:S(2)}, u32[]{:S(2)}) %collective-permute-start.11) | collective-permute-done | bytes 102432 | tf_op jit(solution)/shard_map/ppermute | solution.py:17
  145.3 0.4 maximum_maximum_fusion.2
  145.6 3.7 %fusion.40 = f32[5,32,16,128]{3,2,1,0:T(8,128)S(1)} fusion(f32[5,32,16,128]{3,2,1,0:T(8,128)S(1)} %bitcast.13, f32[5,32,2,128]{3,2,1,0:T(2,128)S(1)} %collective-permute-done.9, f32[5,32,2,128]{3,2,1,0:T(2,128)S(1)} %collective-permute-done.8, f32[5,34,20,128]{3,2,1,0:T(8,128)S(1)} %get-tuple-element.14, f32[5,34,20,128]{3,2,1,0:T(8,128)S(1)} %get-tuple-element.13, ...), kind=kLoop, calls=%fused_computation.85 | loop fusion | flops 14417920 | bytes 8455424 | tf_op jit(solution)/shard_map/add | solution.py:60
  149.7 3.1 %collective-permute-start.13 = (f32[5,32,2,128]{3,2,1,0:T(2,128)S(1)}, f32[5,32,2,128]{3,2,1,0:T(2,128)S(1)}, u32[]{:S(2)}, u32[]{:S(2)}) collective-permute-start(f32[5,32,2,128]{3,2,1,0:T(2,128)S(1)} %get-tuple-element.26), channel_id=1, source_target_pairs={{1,0},{2,1},{3,2},{0,3},{5,4},{6,5},{7,6},{4,7},{9,8},{10,9},{11,1... | collective-permute-start | bytes 491528 | tf_op jit(solution)/shard_map/ppermute | solution.py:17
  152.8 3.9 %collective-permute-done.12 = f32[5,32,2,128]{3,2,1,0:T(2,128)S(1)} collective-permute-done((f32[5,32,2,128]{3,2,1,0:T(2,128)S(1)}, f32[5,32,2,128]{3,2,1,0:T(2,128)S(1)}, u32[]{:S(2)}, u32[]{:S(2)}) %collective-permute-start.12) | collective-permute-done | bytes 163872 | tf_op jit(solution)/shard_map/ppermute | solution.py:15
  156.7 0.7 collective-permute-done.13
  157.4 5.2 %collective-permute-start.14 = (f32[5,2,20,128]{3,2,1,0:T(8,128)S(1)}, f32[5,2,20,128]{3,2,1,0:T(8,128)S(1)}, u32[]{:S(2)}, u32[]{:S(2)}) collective-permute-start(f32[5,2,20,128]{3,2,1,0:T(8,128)S(1)} %get-tuple-element.11), channel_id=1, source_target_pairs={{0,4},{4,8},{8,12},{12,16},{16,20},{20,24},{24,28},{1,5},{5,9},{9,... | collective-permute-start | bytes 307208 | tf_op jit(solution)/shard_map/ppermute | solution.py:15
  162.6 1.9 %collective-permute-start.15 = (f32[5,2,20,128]{3,2,1,0:T(8,128)S(1)}, f32[5,2,20,128]{3,2,1,0:T(8,128)S(1)}, u32[]{:S(2)}, u32[]{:S(2)}) collective-permute-start(f32[5,2,20,128]{3,2,1,0:T(8,128)S(1)} %get-tuple-element.12), channel_id=1, source_target_pairs={{4,0},{8,4},{12,8},{16,12},{20,16},{24,20},{28,24},{5,1},{9,5},{13... | collective-permute-start | bytes 307208 | tf_op jit(solution)/shard_map/ppermute | solution.py:17
  164.5 4.3 %collective-permute-done.15 = f32[5,2,20,128]{3,2,1,0:T(8,128)S(1)} collective-permute-done((f32[5,2,20,128]{3,2,1,0:T(8,128)S(1)}, f32[5,2,20,128]{3,2,1,0:T(8,128)S(1)}, u32[]{:S(2)}, u32[]{:S(2)}) %collective-permute-start.15) | collective-permute-done | bytes 102432 | tf_op jit(solution)/shard_map/ppermute | solution.py:17
  168.8 0.4 maximum_maximum_fusion.3
  169.1 4.6 %fusion.52 = f32[5,32,16,128]{3,2,1,0:T(8,128)} fusion(f32[5,32,16,128]{3,2,1,0:T(8,128)S(1)} %fusion.40, f32[5,32,2,128]{3,2,1,0:T(2,128)S(1)} %collective-permute-done.13, f32[5,32,2,128]{3,2,1,0:T(2,128)S(1)} %collective-permute-done.12, f32[5,34,20,128]{3,2,1,0:T(8,128)S(1)} %get-tuple-element.10, f32[5,34,20,128]{3,2,1,0:T(8,128)S(1)} %get-tuple-element.9, ...), kind=kLoop, calls=%fused_computation.97 | loop fusion | flops 15073280 | bytes 9766144 | tf_op jit(solution)/shard_map/mul | solution.py:61
  (27 shorter events, 2.5 us)
Async XLA Ops:
  1.4 8.2 %collective-permute-start = (f32[5,32,2,128]{3,2,1,0:T(2,128)S(1)}, f32[5,32,2,128]{3,2,1,0:T(2,128)S(1)}, u32[]{:S(2)}, u32[]{:S(2)}) collective-permute-start(f32[5,32,2,128]{3,2,1,0:T(2,128)S(1)} %get-tuple-element.31), channel_id=1, source_target_pairs={{0,1},{1,2},{2,3},{3,0},{4,5},{5,6},{6,7},{7,4},{8,9},{9,10},{10,1... | collective-permute-start | bytes 491528 | tf_op jit(solution)/shard_map/ppermute | solution.py:15
  3.6 9.0 %collective-permute-start.1 = (f32[5,32,2,128]{3,2,1,0:T(2,128)S(1)}, f32[5,32,2,128]{3,2,1,0:T(2,128)S(1)}, u32[]{:S(2)}, u32[]{:S(2)}) collective-permute-start(f32[5,32,2,128]{3,2,1,0:T(2,128)S(1)} %get-tuple-element.32), channel_id=1, source_target_pairs={{1,0},{2,1},{3,2},{0,3},{5,4},{6,5},{7,6},{4,7},{9,8},{10,9},{11,1... | collective-permute-start | bytes 491528 | tf_op jit(solution)/shard_map/ppermute | solution.py:17
  7.4 5.2 %copy-start = (f32[5,32,16,128]{3,2,1,0:T(8,128)S(1)}, f32[5,32,16,128]{3,2,1,0:T(8,128)}, u32[]{:S(2)}) copy-start(f32[5,32,16,128]{3,2,1,0:T(8,128)} %param.5) | copy-start | bytes 3932164
  12.6 6.1 %collective-permute-start.2 = (f32[5,2,20,128]{3,2,1,0:T(8,128)S(1)}, f32[5,2,20,128]{3,2,1,0:T(8,128)S(1)}, u32[]{:S(2)}, u32[]{:S(2)}) collective-permute-start(f32[5,2,20,128]{3,2,1,0:T(8,128)S(1)} %get-tuple-element.23), channel_id=1, source_target_pairs={{0,4},{4,8},{8,12},{12,16},{16,20},{20,24},{24,28},{1,5},{5,9},{9,... | collective-permute-start | bytes 307208 | tf_op jit(solution)/shard_map/ppermute | solution.py:15
  16.8 6.2 %collective-permute-start.3 = (f32[5,2,20,128]{3,2,1,0:T(8,128)S(1)}, f32[5,2,20,128]{3,2,1,0:T(8,128)S(1)}, u32[]{:S(2)}, u32[]{:S(2)}) collective-permute-start(f32[5,2,20,128]{3,2,1,0:T(8,128)S(1)} %get-tuple-element.24), channel_id=1, source_target_pairs={{4,0},{8,4},{12,8},{16,12},{20,16},{24,20},{28,24},{5,1},{9,5},{13... | collective-permute-start | bytes 307208 | tf_op jit(solution)/shard_map/ppermute | solution.py:17
  27.1 7.2 %collective-permute-start.4 = (f32[5,32,2,128]{3,2,1,0:T(2,128)S(1)}, f32[5,32,2,128]{3,2,1,0:T(2,128)S(1)}, u32[]{:S(2)}, u32[]{:S(2)}) collective-permute-start(f32[5,32,2,128]{3,2,1,0:T(2,128)S(1)} %get-tuple-element.29), channel_id=1, source_target_pairs={{0,1},{1,2},{2,3},{3,0},{4,5},{5,6},{6,7},{7,4},{8,9},{9,10},{10,1... | collective-permute-start | bytes 491528 | tf_op jit(solution)/shard_map/ppermute | solution.py:15
  28.0 7.2 %collective-permute-start.5 = (f32[5,32,2,128]{3,2,1,0:T(2,128)S(1)}, f32[5,32,2,128]{3,2,1,0:T(2,128)S(1)}, u32[]{:S(2)}, u32[]{:S(2)}) collective-permute-start(f32[5,32,2,128]{3,2,1,0:T(2,128)S(1)} %get-tuple-element.30), channel_id=1, source_target_pairs={{1,0},{2,1},{3,2},{0,3},{5,4},{6,5},{7,6},{4,7},{9,8},{10,9},{11,1... | collective-permute-start | bytes 491528 | tf_op jit(solution)/shard_map/ppermute | solution.py:17
  35.3 6.5 %collective-permute-start.6 = (f32[5,2,20,128]{3,2,1,0:T(8,128)S(1)}, f32[5,2,20,128]{3,2,1,0:T(8,128)S(1)}, u32[]{:S(2)}, u32[]{:S(2)}) collective-permute-start(f32[5,2,20,128]{3,2,1,0:T(8,128)S(1)} %get-tuple-element.19), channel_id=1, source_target_pairs={{0,4},{4,8},{8,12},{12,16},{16,20},{20,24},{24,28},{1,5},{5,9},{9,... | collective-permute-start | bytes 307208 | tf_op jit(solution)/shard_map/ppermute | solution.py:15
  39.9 6.2 %collective-permute-start.7 = (f32[5,2,20,128]{3,2,1,0:T(8,128)S(1)}, f32[5,2,20,128]{3,2,1,0:T(8,128)S(1)}, u32[]{:S(2)}, u32[]{:S(2)}) collective-permute-start(f32[5,2,20,128]{3,2,1,0:T(8,128)S(1)} %get-tuple-element.20), channel_id=1, source_target_pairs={{4,0},{8,4},{12,8},{16,12},{20,16},{24,20},{28,24},{5,1},{9,5},{13... | collective-permute-start | bytes 307208 | tf_op jit(solution)/shard_map/ppermute | solution.py:17
  51.4 3.7 %copy-start.1 = (s32[32]{0:T(128)S(1)}, s32[32]{0:T(128)}, u32[]{:S(2)}) copy-start(s32[32]{0:T(128)} %param.9) | copy-start | bytes 388
  51.4 32.8 %all-to-all-start = ((f32[5,32,16,128]{3,2,0,1:T(8,128)}), f32[5,32,16,128]{3,2,0,1:T(8,128)S(1)}, u32[]{:S(2)}, u32[]{:S(2)}) async-start(f32[5,32,16,128]{3,2,0,1:T(8,128)} %copy.8), calls=%async_computation | async-start | bytes 2621440 | tf_op jit(solution)/shard_map/all_to_all | solution.py:77
  124.0 7.2 %collective-permute-start.8 = (f32[5,32,2,128]{3,2,1,0:T(2,128)S(1)}, f32[5,32,2,128]{3,2,1,0:T(2,128)S(1)}, u32[]{:S(2)}, u32[]{:S(2)}) collective-permute-start(f32[5,32,2,128]{3,2,1,0:T(2,128)S(1)} %get-tuple-element.27), channel_id=1, source_target_pairs={{0,1},{1,2},{2,3},{3,0},{4,5},{5,6},{6,7},{7,4},{8,9},{9,10},{10,1... | collective-permute-start | bytes 491528 | tf_op jit(solution)/shard_map/ppermute | solution.py:15
  124.1 8.7 %collective-permute-start.9 = (f32[5,32,2,128]{3,2,1,0:T(2,128)S(1)}, f32[5,32,2,128]{3,2,1,0:T(2,128)S(1)}, u32[]{:S(2)}, u32[]{:S(2)}) collective-permute-start(f32[5,32,2,128]{3,2,1,0:T(2,128)S(1)} %get-tuple-element.28), channel_id=1, source_target_pairs={{1,0},{2,1},{3,2},{0,3},{5,4},{6,5},{7,6},{4,7},{9,8},{10,9},{11,1... | collective-permute-start | bytes 491528 | tf_op jit(solution)/shard_map/ppermute | solution.py:17
  132.9 8.1 %collective-permute-start.10 = (f32[5,2,20,128]{3,2,1,0:T(8,128)S(1)}, f32[5,2,20,128]{3,2,1,0:T(8,128)S(1)}, u32[]{:S(2)}, u32[]{:S(2)}) collective-permute-start(f32[5,2,20,128]{3,2,1,0:T(8,128)S(1)} %get-tuple-element.15), channel_id=1, source_target_pairs={{0,4},{4,8},{8,12},{12,16},{16,20},{20,24},{24,28},{1,5},{5,9},{9,... | collective-permute-start | bytes 307208 | tf_op jit(solution)/shard_map/ppermute | solution.py:15
  139.1 6.2 %collective-permute-start.11 = (f32[5,2,20,128]{3,2,1,0:T(8,128)S(1)}, f32[5,2,20,128]{3,2,1,0:T(8,128)S(1)}, u32[]{:S(2)}, u32[]{:S(2)}) collective-permute-start(f32[5,2,20,128]{3,2,1,0:T(8,128)S(1)} %get-tuple-element.16), channel_id=1, source_target_pairs={{4,0},{8,4},{12,8},{16,12},{20,16},{24,20},{28,24},{5,1},{9,5},{13... | collective-permute-start | bytes 307208 | tf_op jit(solution)/shard_map/ppermute | solution.py:17
  149.5 7.2 %collective-permute-start.12 = (f32[5,32,2,128]{3,2,1,0:T(2,128)S(1)}, f32[5,32,2,128]{3,2,1,0:T(2,128)S(1)}, u32[]{:S(2)}, u32[]{:S(2)}) collective-permute-start(f32[5,32,2,128]{3,2,1,0:T(2,128)S(1)} %get-tuple-element.25), channel_id=1, source_target_pairs={{0,1},{1,2},{2,3},{3,0},{4,5},{5,6},{6,7},{7,4},{8,9},{9,10},{10,1... | collective-permute-start | bytes 491528 | tf_op jit(solution)/shard_map/ppermute | solution.py:15
  149.7 7.7 %collective-permute-start.13 = (f32[5,32,2,128]{3,2,1,0:T(2,128)S(1)}, f32[5,32,2,128]{3,2,1,0:T(2,128)S(1)}, u32[]{:S(2)}, u32[]{:S(2)}) collective-permute-start(f32[5,32,2,128]{3,2,1,0:T(2,128)S(1)} %get-tuple-element.26), channel_id=1, source_target_pairs={{1,0},{2,1},{3,2},{0,3},{5,4},{6,5},{7,6},{4,7},{9,8},{10,9},{11,1... | collective-permute-start | bytes 491528 | tf_op jit(solution)/shard_map/ppermute | solution.py:17
  157.4 7.1 %collective-permute-start.14 = (f32[5,2,20,128]{3,2,1,0:T(8,128)S(1)}, f32[5,2,20,128]{3,2,1,0:T(8,128)S(1)}, u32[]{:S(2)}, u32[]{:S(2)}) collective-permute-start(f32[5,2,20,128]{3,2,1,0:T(8,128)S(1)} %get-tuple-element.11), channel_id=1, source_target_pairs={{0,4},{4,8},{8,12},{12,16},{16,20},{20,24},{24,28},{1,5},{5,9},{9,... | collective-permute-start | bytes 307208 | tf_op jit(solution)/shard_map/ppermute | solution.py:15
  162.6 6.2 %collective-permute-start.15 = (f32[5,2,20,128]{3,2,1,0:T(8,128)S(1)}, f32[5,2,20,128]{3,2,1,0:T(8,128)S(1)}, u32[]{:S(2)}, u32[]{:S(2)}) collective-permute-start(f32[5,2,20,128]{3,2,1,0:T(8,128)S(1)} %get-tuple-element.12), channel_id=1, source_target_pairs={{4,0},{8,4},{12,8},{16,12},{20,16},{24,20},{28,24},{5,1},{9,5},{13... | collective-permute-start | bytes 307208 | tf_op jit(solution)/shard_map/ppermute | solution.py:17
where the time goes:
time: 174 us
  waiting for transfers between devices  64.5 us (37%)
  starting transfers between devices  45.6 us (26%)
  blocking collectives  34.3 us (20%)
  other arithmetic  22.7 us (13%)
  local copies, waits for them, and re-layouts  6.18 us (4%)
    all_to_all x1, blocking collectives, shift_rows(): lax.all_to_all(rolled, 'azi', split_axis=2, concat_axis=1, tiled=True)  34.3 us
    all_to_all x1, waiting for transfers between devices, shift_rows(): lax.all_to_all(half, 'azi', split_axis=1, concat_axis=2, tiled=True)  28.9 us
    ppermute x8, starting transfers between devices, with_halo(): lax.ppermute(tail, axis, [(i, (i + 1) % count) for i in range(ends)])  23.4 us
    ppermute x8, waiting for transfers between devices, with_halo(): lax.ppermute(head, axis, [((i + 1) % count, i) for i in range(ends)])  23.2 us
    ppermute x8, starting transfers between devices, with_halo(): lax.ppermute(head, axis, [((i + 1) % count, i) for i in range(ends)])  18.5 us
    ppermute x8, waiting for transfers between devices, with_halo(): lax.ppermute(tail, axis, [(i, (i + 1) % count) for i in range(ends)])  12.4 us
    mul x2, other arithmetic, heun_sections(): 0.5 * (field + first + stencil(extend(first, 2), kappa, speed_r, speed_p))  8.39 us
    add x2, other arithmetic, heun_sections(): first = field + stencil(extend(field, 2), kappa, speed_r, speed_p)  7.34 us
  transfers between devices with their start and end apart: 17, of which 13 were waited for; matrix products, arithmetic and copies ran while one was open for 2% of the time, Pallas kernels for 0%

commit v1 on v0

v1 whole, which is shorter than its diff:
```python
import functools

import jax
import jax.numpy as jnp
from jax import lax
from jax.experimental import pallas as pl
from jax.experimental.pallas import tpu as pltpu
from jax.sharding import PartitionSpec as P

MESH = pl.DeviceIdType.MESH
STAGES = 4
AHEAD = 2


def block_of(rad, azi, n):
    column = rad // 2
    odd = lax.rem(column, 2)
    place = azi + odd * (n - 1 - 2 * azi)
    return column * (2 * n) + 2 * place + lax.rem(rad, 2)


def owner_of(block, n):
    column = block // (2 * n)
    t = lax.rem(block, 2 * n)
    odd = lax.rem(column, 2)
    place = t // 2
    return 2 * column + lax.rem(t, 2), place + odd * (n - 1 - 2 * place)


def kernel(n, blocks, srad, sazi, shifts, fields, kappa, out, x0, x1, x2, x3, adv, kap,
           send1, recv1, send_h, recv_h, send2, recv2):
    count, rows, width = fields.shape[0], fields.shape[1], fields.shape[2]
    own = rows // n
    around = width * n
    depth = fields.shape[3]
    rad, azi = lax.axis_index("rad"), lax.axis_index("azi")
    mine = block_of(rad, azi, n)
    home = mine // n
    spot = lax.rem(mine, n)
    has_prev, has_next = mine > 0, mine < blocks - 1
    prev = owner_of(jnp.maximum(mine - 1, 0), n)
    following = owner_of(jnp.minimum(mine + 1, blocks - 1), n)
    targets = [owner_of(rad * n + b, n) for b in range(n)]
    same = [jnp.logical_and(d[0] == rad, d[1] == azi) for d in targets]
    sources = [(home, jnp.int32(a)) for a in range(n)]
    back = [jnp.logical_and(home == rad, azi == a) for a in range(n)]

    barrier = pltpu.get_barrier_semaphore()
    greeted = jnp.int32(0)
    for device, skip in [*zip(targets, same), *zip(sources, back),
                         (prev, jnp.logical_not(has_prev)), (following, jnp.logical_not(has_next))]:
        @pl.when(jnp.logical_not(skip))
        def _():
            pl.semaphore_signal(barrier, inc=1, device_id=device, device_id_type=MESH)
        greeted = greeted + jnp.where(skip, 0, 1)
    pl.semaphore_wait(barrier, greeted)

    def first_pass(f, act):
        for b in range(n):
            def parts():
                at = pl.ds(azi * width, width)
                if f is None:
                    return kappa.at[pl.ds(b * own, own)], kap.at[:, at], count
                return fields.at[f, pl.ds(b * own, own)], x0.at[f, pl.ds(2, own), at], f

            @pl.when(jnp.logical_not(same[b]))
            def _():
                src, dst, k = parts()
                copy = pltpu.make_async_remote_copy(
                    src, dst, send1.at[k, b], recv1.at[k], device_id=targets[b], device_id_type=MESH)
                copy.start() if act == "start" else copy.wait_send()

            if act == "start":
                @pl.when(same[b])
                def _():
                    src, dst, k = parts()
                    pltpu.make_async_copy(src, dst, recv1.at[k]).start()

    def second_pass(f, act):
        for a in range(n):
            def parts():
                return adv.at[f, :, pl.ds(a * width, width)], out.at[f, pl.ds(spot * own, own)]

            @pl.when(jnp.logical_not(back[a]))
            def _():
                src, dst = parts()
                copy = pltpu.make_async_remote_copy(
                    src, dst, send2.at[f, a], recv2.at[f], device_id=sources[a], device_id_type=MESH)
                copy.start() if act == "start" else copy.wait_send()

            if act == "start":
                @pl.when(back[a])
                def _():
                    src, dst = parts()
                    pltpu.make_async_copy(src, dst, recv2.at[f]).start()

    def halo(x, f, level, act):
        low = pltpu.make_async_remote_copy(
            x.at[f, pl.ds(2, 2)], x.at[f, pl.ds(own + 2, 2)], send_h.at[f, level, 0],
            recv_h.at[f, level, 0], device_id=prev, device_id_type=MESH)
        high = pltpu.make_async_remote_copy(
            x.at[f, pl.ds(own, 2)], x.at[f, pl.ds(0, 2)], send_h.at[f, level, 1],
            recv_h.at[f, level, 1], device_id=following, device_id_type=MESH)

        @pl.when(has_prev)
        def _():
            if act == "start":
                low.start()
            elif act == "send":
                low.wait_send()
            else:
                high.wait_recv()

        @pl.when(has_next)
        def _():
            if act == "start":
                high.start()
            elif act == "send":
                high.wait_send()
            else:
                low.wait_recv()

    lane = lax.broadcasted_iota(jnp.int32, (around, depth), 1)

    def operate(x, f, i):
        u = x[f, i + 2]
        r2m, r1m, r1p, r2p = x[f, i], x[f, i + 1], x[f, i + 3], x[f, i + 4]
        p1p, p1m = pltpu.roll(u, around - 1, 0), pltpu.roll(u, 1, 0)
        p2p, p2m = pltpu.roll(u, around - 2, 0), pltpu.roll(u, 2, 0)
        z1p = jnp.where(lane < depth - 1, pltpu.roll(u, depth - 1, 1), 0.0)
        z1m = jnp.where(lane >= 1, pltpu.roll(u, 1, 1), 0.0)
        z2p = jnp.where(lane < depth - 2, pltpu.roll(u, depth - 2, 1), 0.0)
        z2m = jnp.where(lane >= 2, pltpu.roll(u, 2, 1), 0.0)
        one = (r1p + r1m) + (p1p + p1m) + (z1p + z1m)
        two = (r2p + r2m) + (p2p + p2m) + (z2p + z2m)
        spread = 16.0 * one - two - 90.0 * u
        carried = (srad[f, i] * (8.0 * (r1p - r1m) - (r2p - r2m))
                   + sazi[f, i] * (8.0 * (p1p - p1m) - (p2p - p2m)))
        return u, kap[i] * spread - carried

    def each_row(body):
        def step(i, carry):
            body(i)
            return carry
        lax.fori_loop(0, own, step, 0)

    def clear(f, carry):
        for x in (x0, x1, x2, x3):
            @pl.when(jnp.logical_not(has_prev))
            def _():
                x[f, pl.ds(0, 2)] = jnp.zeros((2, around, depth), jnp.float32)

            @pl.when(jnp.logical_not(has_next))
            def _():
                x[f, pl.ds(own + 2, 2)] = jnp.zeros((2, around, depth), jnp.float32)
        return carry

    first_pass(0, "start")
    first_pass(None, "start")
    for f in range(1, min(AHEAD, count)):
        first_pass(f, "start")
    lax.fori_loop(0, count, clear, 0)
    pltpu.make_async_copy(kap, kap, recv1.at[count]).wait()

    def scale(i):
        kap[i] = kap[i] * (1.0 / 12.0)
    each_row(scale)

    def tick(t, carry):
        def at_stage(lag):
            f = t - lag
            return f, jnp.logical_and(f >= 0, f < count)

        f_next, fine = at_stage(-AHEAD)

        @pl.when(fine)
        def _():
            first_pass(f_next, "start")

        f4, fine4 = at_stage(4)

        @pl.when(fine4)
        def _():
            halo(x3, f4, 3, "recv")

            def body(i):
                u, change = operate(x3, f4, i)
                adv[f4, i] = 0.5 * (x2[f4, i + 2] + u + change)
            each_row(body)
            second_pass(f4, "start")

        f3, fine3 = at_stage(3)

        @pl.when(fine3)
        def _():
            halo(x2, f3, 2, "recv")

            def body(i):
                u, change = operate(x2, f3, i)
                x3[f3, i + 2] = u + change
            each_row(body)
            halo(x3, f3, 3, "start")

        f2, fine2 = at_stage(2)

        @pl.when(fine2)
        def _():
            halo(x1, f2, 1, "recv")

            def body(i):
                u, change = operate(x1, f2, i)
                half = 0.5 * (x0[f2, i + 2] + u + change)
                x2[f2, i + 2] = pltpu.roll(half, shifts[i], 0)
            each_row(body)
            halo(x2, f2, 2, "start")

        f1, fine1 = at_stage(1)

        @pl.when(fine1)
        def _():
            halo(x0, f1, 0, "recv")

            def body(i):
                u, change = operate(x0, f1, i)
                x1[f1, i + 2] = u + change
            each_row(body)
            halo(x1, f1, 1, "start")

        f0, fine0 = at_stage(0)

        @pl.when(fine0)
        def _():
            here = x0.at[f0, pl.ds(2, own)]
            pltpu.make_async_copy(here, here, recv1.at[f0]).wait()
            halo(x0, f0, 0, "start")
        return carry

    lax.fori_loop(0, count + STAGES, tick, 0)

    first_pass(None, "send")

    def finish(f, carry):
        first_pass(f, "send")
        for level, x in enumerate((x0, x1, x2, x3)):
            halo(x, f, level, "send")
        second_pass(f, "send")
        pltpu.make_async_copy(out.at[f], out.at[f], recv2.at[f]).wait()
        return carry
    lax.fori_loop(0, count, finish, 0)


def shards(fields, kappa, radial_speed, azimuth_speed, shifts):
    n = lax.axis_size("azi")
    annuli = lax.axis_size("rad")
    count, rows, width, depth = fields.shape
    own, around = rows // n, width * n
    rad, azi = lax.axis_index("rad"), lax.axis_index("azi")
    mine = block_of(rad, azi, n)
    packed = jnp.concatenate(
        [radial_speed * (1.0 / 12.0), azimuth_speed * (1.0 / 12.0),
         jnp.mod(shifts, around).astype(jnp.float32)[None]], axis=0)
    other = lax.ppermute(packed, "rad", [(i, i ^ 1) for i in range(annuli)])
    rightful = jnp.where(mine // n == rad, packed, other)
    rightful = lax.dynamic_slice_in_dim(rightful, (mine % n) * own, own, axis=1)
    srad, sazi = rightful[:count], rightful[count:2 * count]
    turn = rightful[2 * count].astype(jnp.int32)

    tall = pltpu.VMEM((count, own + 4, around, depth), jnp.float32)
    held = 4 * count * around * depth * (4 * (own + 4) + own + own)
    any_space = pl.BlockSpec(memory_space=pl.ANY)
    small = pl.BlockSpec(memory_space=pltpu.SMEM)
    return pl.pallas_call(
        functools.partial(kernel, n, n * annuli),
        out_shape=jax.ShapeDtypeStruct(fields.shape, jnp.float32),
        in_specs=[small, small, small, any_space, any_space],
        out_specs=any_space,
        scratch_shapes=[
            tall, tall, tall, tall,
            pltpu.VMEM((count, own, around, depth), jnp.float32),
            pltpu.VMEM((own, around, depth), jnp.float32),
            pltpu.SemaphoreType.DMA((count + 1, n)),
            pltpu.SemaphoreType.DMA((count + 1,)),
            pltpu.SemaphoreType.DMA((count, STAGES, 2)),
            pltpu.SemaphoreType.DMA((count, STAGES, 2)),
            pltpu.SemaphoreType.DMA((count, n)),
            pltpu.SemaphoreType.DMA((count,)),
        ],
        compiler_params=pltpu.CompilerParams(
            collective_id=0, has_side_effects=True, vmem_limit_bytes=held + (8 << 20)),
    )(srad, sazi, turn, fields, kappa)


def solution(mesh):
    placed = (
        P(None, "rad", "azi", None),
        P("rad", "azi", None),
        P(None, "rad"),
        P(None, "rad"),
        P("rad"),
    )
    return jax.shard_map(
        shards, mesh=mesh, in_specs=placed, out_specs=P(None, "rad", "azi", None), check_vma=False
    )
```

time: 174 us -> 95.6 us (0.55)
  Pallas kernels: 0 us -> 87.8 us
  waiting for transfers between devices: 64.5 us -> 1.1 us
  starting transfers between devices: 45.6 us -> 0.12 us
  blocking collectives: 34.3 us -> 0 us
  other arithmetic: 22.7 us -> 1.46 us
  local copies, waits for them, and re-layouts: 6.18 us -> 3.32 us
    pallas_call x0 -> x1, Pallas kernels: none -> 87.8 us  [shards(): pl.pallas_call(functools.partial(kernel, n, n * annuli), out_shape=jax.Sh...]
    ppermute x16 -> x1, starting transfers between devices: 42 us -> 0.12 us  [shards(): other = lax.ppermute(packed, 'rad', [(i, i ^ 1) for i in range(annuli)])]
    ppermute x16 -> x1, waiting for transfers between devices: 35.5 us -> 1.1 us  [shards(): other = lax.ppermute(packed, 'rad', [(i, i ^ 1) for i in range(annuli)])]
    all_to_all x1 -> x0, blocking collectives: 34.3 us -> none  [shift_rows(): lax.all_to_all(rolled, 'azi', split_axis=2, concat_axis=1, tiled=True)]
    all_to_all x1 -> x0, waiting for transfers between devices: 28.9 us -> none  [shift_rows(): lax.all_to_all(half, 'azi', split_axis=1, concat_axis=2, tiled=True)]
    mul x4 -> x1, other arithmetic: 10.1 us -> 0.71 us  [shards(): azimuth_speed * (1.0 / 12.0)]
    add x2 -> x0, other arithmetic: 7.34 us -> none  [heun_sections(): first = field + stencil(extend(field, 2), kappa, speed_r, speed_p)]
    all_to_all x1 -> x0, starting transfers between devices: 3.67 us -> none  [shift_rows(): lax.all_to_all(half, 'azi', split_axis=1, concat_axis=2, tiled=True)]
  transfers between devices with their start and end apart: 17 -> 1, of which waited for: 13 -> 1; matrix products, arithmetic and copies ran while one was open for 2% -> 0% of each run, Pallas kernels for 0% -> 0%
where the time goes in v1:
time: 95.6 us; the launch traced here: 93.9 us
  Pallas kernels  87.8 us (92%)
  local copies, waits for them, and re-layouts  3.32 us (3%)
  other arithmetic  1.46 us (2%)
  waiting for transfers between devices  1.1 us (1%)
    pallas_call x1, Pallas kernels, shards(): pl.pallas_call(functools.partial(kernel, n, n * annuli), out_shape=jax.Sh...  87.8 us
    unnamed x5, local copies, waits for them, and re-layouts  3.32 us
  transfers between devices with their start and end apart: 1, of which 1 were waited for; matrix products, arithmetic and copies ran while one was open for 0% of the time, Pallas kernels for 0%

profile of v1, /device:TPU:1, one launch (start us, length us, event | category | flops | bytes accessed | tf_op | source)
XLA Modules:
  0.0 93.9 jit_solution(3429235706595300968)
XLA Ops:
  0.0 0.7 fusion.1
  0.7 0.7 broadcast_multiply_fusion
  1.4 0.1 collective-permute-start
  1.5 1.1 %collective-permute-done = f32[11,32]{1,0:T(8,128)S(1)} collective-permute-done((f32[11,32]{1,0:T(8,128)S(1)}, f32[11,32]{1,0:T(8,128)S(1)}, u32[]{:S(2)}, u32[]{:S(2)}) %collective-permute-start) | collective-permute-done | bytes 1440 | tf_op jit(solution)/shard_map/ppermute | solution.py:262
  2.6 0.1 dynamic-slice_select_fusion
  2.7 0.0 copy-start
  2.7 1.3 %copy-done = f32[5,32,16,128]{3,2,1,0:T(8,128)S(1)} copy-done((f32[5,32,16,128]{3,2,1,0:T(8,128)S(1)}, f32[5,32,16,128]{3,2,1,0:T(8,128)}, u32[]{:S(2)}) %copy-start) | copy-done | bytes 1310744
  4.0 0.0 copy-start.1
  4.0 0.9 %copy-done.1 = f32[32,16,128]{2,1,0:T(8,128)S(1)} copy-done((f32[32,16,128]{2,1,0:T(8,128)S(1)}, f32[32,16,128]{2,1,0:T(8,128)}, u32[]{:S(2)}) %copy-start.1) | copy-done | bytes 262168
  5.0 87.8 %shard_map.55 = f32[5,32,16,128]{3,2,1,0:T(8,128)S(1)} custom-call(f32[5,8]{1,0:T(8,128)S(1)} %get-tuple-element.6.srad, f32[5,8]{1,0:T(8,128)S(1)} %get-tuple-element.5.sazi, s32[8]{0:T(128)S(1)} %fusion.3.shifts, f32[5,32,16,128]{3,2,1,0:T(8,128)S(1)} %copy-done, f32[32,16,128]{2,1,0:T(8,128)S(1)} %copy-done.1), custom_call_target="tpu_custom_call" | custom-call | tf_op jit(solution)/shard_map/pallas_call | solution.py:272
  92.8 1.1 %copy.7 = f32[5,32,16,128]{3,2,1,0:T(8,128)} copy(f32[5,32,16,128]{3,2,1,0:T(8,128)S(1)} %shard_map.55) | data formatting | bytes 2621440
  (3 shorter events, 0.0 us)
Async XLA Ops:
  1.4 1.2 %collective-permute-start = (f32[11,32]{1,0:T(8,128)S(1)}, f32[11,32]{1,0:T(8,128)S(1)}, u32[]{:S(2)}, u32[]{:S(2)}) collective-permute-start(f32[11,32]{1,0:T(8,128)S(1)} %pad_maximum_fusion), channel_id=1, source_target_pairs={{0,4},{4,0},{8,12},{12,8},{16,20},{20,16},{24,28},{28,24},{1,5},{5... | collective-permute-start | bytes 4232 | tf_op jit(solution)/shard_map/ppermute | solution.py:262
  2.7 1.3 %copy-start = (f32[5,32,16,128]{3,2,1,0:T(8,128)S(1)}, f32[5,32,16,128]{3,2,1,0:T(8,128)}, u32[]{:S(2)}) copy-start(f32[5,32,16,128]{3,2,1,0:T(8,128)} %fields.1) | copy-start | bytes 3932164
  4.0 0.9 %copy-start.1 = (f32[32,16,128]{2,1,0:T(8,128)S(1)}, f32[32,16,128]{2,1,0:T(8,128)}, u32[]{:S(2)}) copy-start(f32[32,16,128]{2,1,0:T(8,128)} %kappa.1) | copy-start | bytes 786436

commit v2 on v1

--- a/solution.py
+++ b/solution.py
@@ -8,6 +8,7 @@
 from jax.sharding import PartitionSpec as P
 
 MESH = pl.DeviceIdType.MESH
+HALO = 8
 STAGES = 4
 AHEAD = 2
 
@@ -28,6 +29,254 @@
 
 
 def kernel(n, blocks, srad, sazi, shifts, fields, kappa, out, x0, x1, x2, x3, adv, kap,
+           send1, recv1, send_x, recv_x, send_h, recv_h, send2, recv2):
+    count, rows, width, depth = fields.shape
+    own = rows // n
+    around = width * n
+    rad, azi = lax.axis_index("rad"), lax.axis_index("azi")
+    core = lax.rem(rad, 2)
+    mine = block_of(rad, azi, n)
+    home = mine // n
+    spot = lax.rem(mine, n)
+    turn = lax.rem(mine, 2 * n)
+    middle = jnp.logical_or(turn == n, turn == n - 1)
+    has_prev, has_next = mine > 0, mine < blocks - 1
+    from_prev = jnp.logical_and(has_prev, turn != n)
+    from_next = jnp.logical_and(has_next, turn != n - 1)
+    prev = owner_of(jnp.maximum(mine - 1, 0), n)
+    following = owner_of(jnp.minimum(mine + 1, blocks - 1), n)
+
+    def is_me(device):
+        return jnp.logical_and(device[0] == rad, device[1] == azi)
+
+    targets = [owner_of(rad * n + b, n) for b in range(n)]
+    same = [is_me(d) for d in targets]
+    sources = [(home, jnp.int32(a)) for a in range(n)]
+    back = [is_me(d) for d in sources]
+    across = owner_of(rad * n + n - core * (n + 1), n)
+    across_same = is_me(across)
+    holders = [(home + 1 - 2 * lax.rem(home, 2), jnp.int32(a)) for a in range(n)]
+    not_held = [jnp.logical_or(jnp.logical_not(middle), is_me(d)) for d in holders]
+
+    barrier = pltpu.get_barrier_semaphore()
+    greeted = jnp.int32(0)
+    for device, skip in [*zip(targets, same), *zip(sources, back), (across, across_same),
+                         *zip(holders, not_held), (prev, jnp.logical_not(from_prev)),
+                         (following, jnp.logical_not(from_next))]:
+        @pl.when(jnp.logical_not(skip))
+        def _():
+            pl.semaphore_signal(barrier, inc=1, device_id=device, device_id_type=MESH)
+        greeted = greeted + jnp.where(skip, 0, 1)
+    pl.semaphore_wait(barrier, greeted)
+
+    def move(act, src, dst, send, recv, device, local):
+        @pl.when(jnp.logical_not(local))
+        def _():
+            copy = pltpu.make_async_remote_copy(
+                src, dst, send, recv, device_id=device, device_id_type=MESH)
+            copy.start() if act == "start" else copy.wait_send()
+
+        if act == "start":
+            @pl.when(local)
+            def _():
+                pltpu.make_async_copy(src, dst, recv).start()
+
+    def held(q):
+        return kappa if isinstance(q, int) else fields.at[q - 1]
+
+    def first_pass(q, act):
+        at = pl.ds(azi * width, width)
+        edge = (1 - core) * (rows - HALO)
+        move(act, held(q).at[pl.ds(edge, HALO)], x0.at[q, pl.ds(core * (HALO + own), HALO), at],
+             send_x.at[q], recv_x.at[q], across, across_same)
+        for b in range(n):
+            move(act, held(q).at[pl.ds(b * own, own)], x0.at[q, pl.ds(HALO, own), at],
+                 send1.at[q, b], recv1.at[q], targets[b], same[b])
+
+    def second_pass(f, act):
+        for a in range(n):
+            move(act, adv.at[f, :, pl.ds(a * width, width)], out.at[f, pl.ds(spot * own, own)],
+                 send2.at[f, a], recv2.at[f], sources[a], back[a])
+
+    def halo(q, act):
+        low = pltpu.make_async_remote_copy(
+            x0.at[q, pl.ds(HALO, HALO)], x0.at[q, pl.ds(own + HALO, HALO)], send_h.at[q, 0],
+            recv_h.at[q, 0], device_id=prev, device_id_type=MESH)
+        high = pltpu.make_async_remote_copy(
+            x0.at[q, pl.ds(own, HALO)], x0.at[q, pl.ds(0, HALO)], send_h.at[q, 1],
+            recv_h.at[q, 1], device_id=following, device_id_type=MESH)
+
+        @pl.when(from_prev)
+        def _():
+            if act == "start":
+                low.start()
+            elif act == "send":
+                low.wait_send()
+            else:
+                high.wait_recv()
+
+        @pl.when(from_next)
+        def _():
+            if act == "start":
+                high.start()
+            elif act == "send":
+                high.wait_send()
+            else:
+                low.wait_recv()
+
+        if act == "recv":
+            @pl.when(middle)
+            def _():
+                here = x0.at[q, pl.ds(0, HALO)]
+                pltpu.make_async_copy(here, here, recv_x.at[q]).wait()
+
+    lane = lax.broadcasted_iota(jnp.int32, (around, depth), 1)
+
+    def operate(x, f, i, row):
+        u = x[i + 2]
+        r2m, r1m, r1p, r2p = x[i], x[i + 1], x[i + 3], x[i + 4]
+        p1p, p1m = pltpu.roll(u, around - 1, 0), pltpu.roll(u, 1, 0)
+        p2p, p2m = pltpu.roll(u, around - 2, 0), pltpu.roll(u, 2, 0)
+        z1p = jnp.where(lane < depth - 1, pltpu.roll(u, depth - 1, 1), 0.0)
+        z1m = jnp.where(lane >= 1, pltpu.roll(u, 1, 1), 0.0)
+        z2p = jnp.where(lane < depth - 2, pltpu.roll(u, depth - 2, 1), 0.0)
+        z2m = jnp.where(lane >= 2, pltpu.roll(u, 2, 1), 0.0)
+        one = (r1p + r1m) + (p1p + p1m) + (z1p + z1m)
+        two = (r2p + r2m) + (p2p + p2m) + (z2p + z2m)
+        spread = 16.0 * one - two - 90.0 * u
+        carried = (srad[f, row] * (8.0 * (r1p - r1m) - (r2p - r2m))
+                   + sazi[f, row] * (8.0 * (p1p - p1m) - (p2p - p2m)))
+        return u, kap[row] * spread - carried
+
+    def each_row(length, body):
+        def step(i, carry):
+            body(i)
+            return carry
+        lax.fori_loop(0, length, step, 0)
+
+    def clear(q, carry):
+        @pl.when(jnp.logical_not(has_prev))
+        def _():
+            x0[q, pl.ds(0, HALO)] = jnp.zeros((HALO, around, depth), jnp.float32)
+
+        @pl.when(jnp.logical_not(has_next))
+        def _():
+            x0[q, pl.ds(own + HALO, HALO)] = jnp.zeros((HALO, around, depth), jnp.float32)
+        return carry
+
+    def pass_on(q):
+        here = x0.at[q, pl.ds(HALO, own)]
+        pltpu.make_async_copy(here, here, recv1.at[q]).wait()
+        halo(q, "start")
+
+    def begin(q, carry):
+        first_pass(q, "start")
+        return carry
+
+    first_pass(0, "start")
+    lax.fori_loop(1, count + 1, begin, 0)
+    lax.fori_loop(0, count + 1, clear, 0)
+    pass_on(0)
+    halo(0, "recv")
+
+    def scale(i):
+        kap[i] = x0[0, i] * (1.0 / 12.0)
+    each_row(own + 2 * HALO, scale)
+
+    def tick(t, carry):
+        @pl.when(t <= count)
+        def _():
+            pass_on(t)
+
+        @pl.when(t >= 2)
+        def _():
+            q = t - 1
+            f = q - 1
+            halo(q, "recv")
+            base = x0.at[q]
+
+            def body1(i):
+                u, change = operate(base, f, i, i + 2)
+                x1[i] = u + change
+            each_row(own + 2 * HALO - 4, body1)
+
+            def body2(i):
+                u, change = operate(x1, f, i, i + 4)
+                half = 0.5 * (base[i + 4] + u + change)
+                x2[i] = pltpu.roll(half, shifts[i + 4], 0)
+            each_row(own + 2 * HALO - 8, body2)
+
+            def body3(i):
+                u, change = operate(x2, f, i, i + 6)
+                x3[i] = u + change
+            each_row(own + 2 * HALO - 12, body3)
+
+            def body4(i):
+                u, change = operate(x3, f, i, i + 8)
+                adv[f, i] = 0.5 * (x2[i + 4] + u + change)
+            each_row(own, body4)
+            second_pass(f, "start")
+        return carry
+
+    lax.fori_loop(1, count + 2, tick, 0)
+
+    first_pass(0, "send")
+    halo(0, "send")
+
+    def finish(f, carry):
+        first_pass(f + 1, "send")
+        halo(f + 1, "send")
+        second_pass(f, "send")
+        pltpu.make_async_copy(out.at[f], out.at[f], recv2.at[f]).wait()
+        return carry
+    lax.fori_loop(0, count, finish, 0)
+
+
+def shards(fields, kappa, radial_speed, azimuth_speed, shifts):
+    n = lax.axis_size("azi")
+    annuli = lax.axis_size("rad")
+    count, rows, width, depth = fields.shape
+    own, around = rows // n, width * n
+    if own < HALO or n % 2:
+        return shards_by_steps(fields, kappa, radial_speed, azimuth_speed, shifts)
+    rad, azi = lax.axis_index("rad"), lax.axis_index("azi")
+    mine = block_of(rad, azi, n)
+    packed = jnp.concatenate(
+        [radial_speed * (1.0 / 12.0), azimuth_speed * (1.0 / 12.0),
+         jnp.mod(shifts, around).astype(jnp.float32)[None]], axis=0)
+    below = lax.ppermute(packed, "rad", [(i, i + 1) for i in range(annuli - 1)])
+    above = lax.ppermute(packed, "rad", [(i + 1, i) for i in range(annuli - 1)])
+    wide = jnp.concatenate([below, packed, above], axis=1)
+    start = mine * own - HALO - (rad - 1) * rows
+    tall = own + 2 * HALO
+    wide = lax.dynamic_slice_in_dim(wide, start, tall, axis=1)
+    srad, sazi = wide[:count], wide[count:2 * count]
+    turn = wide[2 * count].astype(jnp.int32)
+
+    def scratch(*lead):
+        return pltpu.VMEM((*lead, around, depth), jnp.float32)
+
+    held = 4 * around * depth * ((count + 2) * tall + 3 * tall + count * own)
+    any_space = pl.BlockSpec(memory_space=pl.ANY)
+    small = pl.BlockSpec(memory_space=pltpu.SMEM)
+    dma = pltpu.SemaphoreType.DMA
+    return pl.pallas_call(
+        functools.partial(kernel, n, n * annuli),
+        out_shape=jax.ShapeDtypeStruct(fields.shape, jnp.float32),
+        in_specs=[small, small, small, any_space, any_space],
+        out_specs=any_space,
+        scratch_shapes=[
+            scratch(count + 1, tall), scratch(tall - 4), scratch(tall - 8), scratch(tall - 12),
+            scratch(count, own), scratch(tall),
+            dma((count + 1, n)), dma((count + 1,)), dma((count + 1,)), dma((count + 1,)),
+            dma((count + 1, 2)), dma((count + 1, 2)), dma((count, n)), dma((count,)),
+        ],
+        compiler_params=pltpu.CompilerParams(
+            collective_id=0, has_side_effects=True, vmem_limit_bytes=held + (8 << 20)),
+    )(srad, sazi, turn, fields, kappa)
+
+
+def kernel_by_steps(n, blocks, srad, sazi, shifts, fields, kappa, out, x0, x1, x2, x3, adv, kap,
            send1, recv1, send_h, recv_h, send2, recv2):
     count, rows, width = fields.shape[0], fields.shape[1], fields.shape[2]
     own = rows // n
@@ -249,7 +498,7 @@
     lax.fori_loop(0, count, finish, 0)
 
 
-def shards(fields, kappa, radial_speed, azimuth_speed, shifts):
+def shards_by_steps(fields, kappa, radial_speed, azimuth_speed, shifts):
     n = lax.axis_size("azi")
     annuli = lax.axis_size("rad")
     count, rows, width, depth = fields.shape
@@ -270,7 +519,7 @@
     any_space = pl.BlockSpec(memory_space=pl.ANY)
     small = pl.BlockSpec(memory_space=pltpu.SMEM)
     return pl.pallas_call(
-        functools.partial(kernel, n, n * annuli),
+        functools.partial(kernel_by_steps, n, n * annuli),
         out_shape=jax.ShapeDtypeStruct(fields.shape, jnp.float32),
         in_specs=[small, small, small, any_space, any_space],
         out_specs=any_space,
@@ -286,7 +535,7 @@
             pltpu.SemaphoreType.DMA((count,)),
         ],
         compiler_params=pltpu.CompilerParams(
-            collective_id=0, has_side_effects=True, vmem_limit_bytes=held + (8 << 20)),
+            collective_id=1, has_side_effects=True, vmem_limit_bytes=held + (8 << 20)),
     )(srad, sazi, turn, fields, kappa)
 
 

time: 95.6 us -> 104 us (1.088)
  the two profiles are of different devices: /device:TPU:1 before, /device:TPU:4 now
where the time goes in v2:
time: 104 us
  Pallas kernels  90.1 us (87%)
  starting transfers between devices  4.7 us (5%)
  waiting for transfers between devices  3.9 us (4%)
  local copies, waits for them, and re-layouts  3.32 us (3%)
  other arithmetic  1.47 us (1%)
    pallas_call x1, Pallas kernels, shards(): pl.pallas_call(functools.partial(kernel, n, n * annuli), out_shape=jax.Sh...  90.1 us
    ppermute x1, waiting for transfers between devices, shards(): below = lax.ppermute(packed, 'rad', [(i, i + 1) for i in range(annuli - 1)])  3.9 us
    unnamed x5, local copies, waits for them, and re-layouts  3.32 us
    ppermute x1, starting transfers between devices, shards(): above = lax.ppermute(packed, 'rad', [(i + 1, i) for i in range(annuli - 1)])  2.78 us
  transfers between devices with their start and end apart: 2, of which 1 were waited for; matrix products, arithmetic and copies ran while one was open for 0% of the time, Pallas kernels for 0%

profile of v2, /device:TPU:4, one launch (start us, length us, event | category | flops | bytes accessed | tf_op | source)
XLA Modules:
  0.0 103.6 jit_solution(14864719563336642923)
XLA Ops:
  0.0 0.7 fusion.1
  0.7 0.7 broadcast_multiply_fusion
  1.4 2.8 %collective-permute-start.1 = (f32[11,32]{1,0:T(8,128)S(1)}, f32[11,32]{1,0:T(8,128)S(1)}, u32[]{:S(2)}, u32[]{:S(2)}) collective-permute-start(f32[11,32]{1,0:T(8,128)S(1)} %pad_maximum_fusion), channel_id=1, source_target_pairs={{4,0},{8,4},{12,8},{16,12},{20,16},{24,20},{28,24},{5,1},{9,5},{13... | collective-permute-start | bytes 4232 | tf_op jit(solution)/shard_map/ppermute | solution.py:248
  4.2 1.9 %collective-permute-start = (f32[11,32]{1,0:T(8,128)S(1)}, f32[11,32]{1,0:T(8,128)S(1)}, u32[]{:S(2)}, u32[]{:S(2)}) collective-permute-start(f32[11,32]{1,0:T(8,128)S(1)} %pad_maximum_fusion), channel_id=1, source_target_pairs={{0,4},{4,8},{8,12},{12,16},{16,20},{20,24},{24,28},{1,5},{5,9},{9,... | collective-permute-start | bytes 4232 | tf_op jit(solution)/shard_map/ppermute | solution.py:247
  6.1 0.0 collective-permute-done.1
  6.1 3.9 %collective-permute-done = f32[11,32]{1,0:T(8,128)S(1)} collective-permute-done((f32[11,32]{1,0:T(8,128)S(1)}, f32[11,32]{1,0:T(8,128)S(1)}, u32[]{:S(2)}, u32[]{:S(2)}) %collective-permute-start) | collective-permute-done | bytes 1440 | tf_op jit(solution)/shard_map/ppermute | solution.py:247
  10.0 0.1 dynamic-slice_maximum_fusion
  10.2 0.0 copy-start
  10.2 1.3 %copy-done = f32[5,32,16,128]{3,2,1,0:T(8,128)S(1)} copy-done((f32[5,32,16,128]{3,2,1,0:T(8,128)S(1)}, f32[5,32,16,128]{3,2,1,0:T(8,128)}, u32[]{:S(2)}) %copy-start) | copy-done | bytes 1310744
  11.5 0.0 copy-start.1
  11.5 0.9 copy-done.1
  12.4 90.1 %shard_map.55 = f32[5,32,16,128]{3,2,1,0:T(8,128)S(1)} custom-call(f32[5,24]{1,0:T(8,128)S(1)} %get-tuple-element.6.srad, f32[5,24]{1,0:T(8,128)S(1)} %get-tuple-element.5.sazi, s32[24]{0:T(128)S(1)} %fusion.3.shifts, f32[5,32,16,128]{3,2,1,0:T(8,128)S(1)} %copy-done, f32[32,16,128]{2,1,0:T(8,128)S(1)} %copy-done.1), custom_call_target="tpu_custom_call" | custom-call | tf_op jit(solution)/shard_map/pallas_call | solution.py:263
  102.5 1.1 %copy.7 = f32[5,32,16,128]{3,2,1,0:T(8,128)} copy(f32[5,32,16,128]{3,2,1,0:T(8,128)S(1)} %shard_map.55) | data formatting | bytes 2621440
  (3 shorter events, 0.0 us)
Async XLA Ops:
  1.4 4.8 %collective-permute-start.1 = (f32[11,32]{1,0:T(8,128)S(1)}, f32[11,32]{1,0:T(8,128)S(1)}, u32[]{:S(2)}, u32[]{:S(2)}) collective-permute-start(f32[11,32]{1,0:T(8,128)S(1)} %pad_maximum_fusion), channel_id=1, source_target_pairs={{4,0},{8,4},{12,8},{16,12},{20,16},{24,20},{28,24},{5,1},{9,5},{13... | collective-permute-start | bytes 4232 | tf_op jit(solution)/shard_map/ppermute | solution.py:248
  4.2 5.9 %collective-permute-start = (f32[11,32]{1,0:T(8,128)S(1)}, f32[11,32]{1,0:T(8,128)S(1)}, u32[]{:S(2)}, u32[]{:S(2)}) collective-permute-start(f32[11,32]{1,0:T(8,128)S(1)} %pad_maximum_fusion), channel_id=1, source_target_pairs={{0,4},{4,8},{8,12},{12,16},{16,20},{20,24},{24,28},{1,5},{5,9},{9,... | collective-permute-start | bytes 4232 | tf_op jit(solution)/shard_map/ppermute | solution.py:247
  10.2 1.3 %copy-start = (f32[5,32,16,128]{3,2,1,0:T(8,128)S(1)}, f32[5,32,16,128]{3,2,1,0:T(8,128)}, u32[]{:S(2)}) copy-start(f32[5,32,16,128]{3,2,1,0:T(8,128)} %fields.1) | copy-start | bytes 3932164
  11.5 0.9 copy-start.1

commit v3 on v2

--- a/solution.py
+++ b/solution.py
@@ -11,6 +11,7 @@
 HALO = 8
 STAGES = 4
 AHEAD = 2
+GROUP = 4
 
 
 def block_of(rad, azi, n):
@@ -148,11 +149,15 @@
                    + sazi[f, row] * (8.0 * (p1p - p1m) - (p2p - p2m)))
         return u, kap[row] * spread - carried
 
-    def each_row(length, body):
+    def each_row(length, value, dst):
+        group = next(k for k in (GROUP, 2, 1) if length % k == 0)
+
         def step(i, carry):
-            body(i)
+            at = [i * group + k for k in range(group)]
+            for k, result in [(k, value(k)) for k in at]:
+                dst[k] = result
             return carry
-        lax.fori_loop(0, length, step, 0)
+        lax.fori_loop(0, length // group, step, 0)
 
     def clear(q, carry):
         @pl.when(jnp.logical_not(has_prev))
@@ -174,16 +179,18 @@
         return carry
 
     first_pass(0, "start")
-    lax.fori_loop(1, count + 1, begin, 0)
+    lax.fori_loop(1, min(AHEAD, count) + 1, begin, 0)
     lax.fori_loop(0, count + 1, clear, 0)
     pass_on(0)
     halo(0, "recv")
 
-    def scale(i):
-        kap[i] = x0[0, i] * (1.0 / 12.0)
-    each_row(own + 2 * HALO, scale)
+    each_row(own + 2 * HALO, lambda i: x0[0, i] * (1.0 / 12.0), kap)
 
     def tick(t, carry):
+        @pl.when(t + AHEAD <= count)
+        def _():
+            first_pass(t + AHEAD, "start")
+
         @pl.when(t <= count)
         def _():
             pass_on(t)
@@ -195,26 +202,26 @@
             halo(q, "recv")
             base = x0.at[q]
 
-            def body1(i):
+            def value1(i):
                 u, change = operate(base, f, i, i + 2)
-                x1[i] = u + change
-            each_row(own + 2 * HALO - 4, body1)
-
-            def body2(i):
+                return u + change
+            each_row(own + 2 * HALO - 4, value1, x1)
+
+            def value2(i):
                 u, change = operate(x1, f, i, i + 4)
                 half = 0.5 * (base[i + 4] + u + change)
-                x2[i] = pltpu.roll(half, shifts[i + 4], 0)
-            each_row(own + 2 * HALO - 8, body2)
-
-            def body3(i):
+                return pltpu.roll(half, shifts[i + 4], 0)
+            each_row(own + 2 * HALO - 8, value2, x2)
+
+            def value3(i):
                 u, change = operate(x2, f, i, i + 6)
-                x3[i] = u + change
-            each_row(own + 2 * HALO - 12, body3)
-
-            def body4(i):
+                return u + change
+            each_row(own + 2 * HALO - 12, value3, x3)
+
+            def value4(i):
                 u, change = operate(x3, f, i, i + 8)
-                adv[f, i] = 0.5 * (x2[i + 4] + u + change)
-            each_row(own, body4)
+                return 0.5 * (x2[i + 4] + u + change)
+            each_row(own, value4, adv.at[f])
             second_pass(f, "start")
         return carry
 

time: 104 us -> 96.1 us (0.924)
  the two profiles are of different devices: /device:TPU:4 before, /device:TPU:28 now
where the time goes in v3:
time: 96.1 us; the launch traced here: 95.8 us
  Pallas kernels  82.3 us (86%)
  starting transfers between devices  4.7 us (5%)
  waiting for transfers between devices  3.9 us (4%)
  local copies, waits for them, and re-layouts  3.32 us (3%)
  other arithmetic  1.47 us (2%)
    pallas_call x1, Pallas kernels, shards(): pl.pallas_call(functools.partial(kernel, n, n * annuli), out_shape=jax.Sh...  82.3 us
    ppermute x1, waiting for transfers between devices, shards(): below = lax.ppermute(packed, 'rad', [(i, i + 1) for i in range(annuli - 1)])  3.9 us
    unnamed x5, local copies, waits for them, and re-layouts  3.32 us
    ppermute x1, starting transfers between devices, shards(): above = lax.ppermute(packed, 'rad', [(i + 1, i) for i in range(annuli - 1)])  2.78 us
  transfers between devices with their start and end apart: 2, of which 1 were waited for; matrix products, arithmetic and copies ran while one was open for 0% of the time, Pallas kernels for 0%

profile of v3, /device:TPU:28, one launch (start us, length us, event | category | flops | bytes accessed | tf_op | source)
XLA Modules:
  0.0 95.8 jit_solution(6031247016517065309)
XLA Ops:
  0.0 0.7 fusion.1
  0.7 0.7 broadcast_multiply_fusion
  1.4 2.8 %collective-permute-start.1 = (f32[11,32]{1,0:T(8,128)S(1)}, f32[11,32]{1,0:T(8,128)S(1)}, u32[]{:S(2)}, u32[]{:S(2)}) collective-permute-start(f32[11,32]{1,0:T(8,128)S(1)} %pad_maximum_fusion), channel_id=1, source_target_pairs={{4,0},{8,4},{12,8},{16,12},{20,16},{24,20},{28,24},{5,1},{9,5},{13... | collective-permute-start | bytes 4232 | tf_op jit(solution)/shard_map/ppermute | solution.py:255
  4.2 1.9 %collective-permute-start = (f32[11,32]{1,0:T(8,128)S(1)}, f32[11,32]{1,0:T(8,128)S(1)}, u32[]{:S(2)}, u32[]{:S(2)}) collective-permute-start(f32[11,32]{1,0:T(8,128)S(1)} %pad_maximum_fusion), channel_id=1, source_target_pairs={{0,4},{4,8},{8,12},{12,16},{16,20},{20,24},{24,28},{1,5},{5,9},{9,... | collective-permute-start | bytes 4232 | tf_op jit(solution)/shard_map/ppermute | solution.py:254
  6.1 0.0 collective-permute-done.1
  6.1 3.9 %collective-permute-done = f32[11,32]{1,0:T(8,128)S(1)} collective-permute-done((f32[11,32]{1,0:T(8,128)S(1)}, f32[11,32]{1,0:T(8,128)S(1)}, u32[]{:S(2)}, u32[]{:S(2)}) %collective-permute-start) | collective-permute-done | bytes 1440 | tf_op jit(solution)/shard_map/ppermute | solution.py:254
  10.0 0.1 dynamic-slice_maximum_fusion
  10.2 0.0 copy-start
  10.2 1.3 %copy-done = f32[5,32,16,128]{3,2,1,0:T(8,128)S(1)} copy-done((f32[5,32,16,128]{3,2,1,0:T(8,128)S(1)}, f32[5,32,16,128]{3,2,1,0:T(8,128)}, u32[]{:S(2)}) %copy-start) | copy-done | bytes 1310744
  11.5 0.0 copy-start.1
  11.5 0.9 copy-done.1
  12.4 82.3 %shard_map.55 = f32[5,32,16,128]{3,2,1,0:T(8,128)S(1)} custom-call(f32[5,24]{1,0:T(8,128)S(1)} %get-tuple-element.6.srad, f32[5,24]{1,0:T(8,128)S(1)} %get-tuple-element.5.sazi, s32[24]{0:T(128)S(1)} %fusion.3.shifts, f32[5,32,16,128]{3,2,1,0:T(8,128)S(1)} %copy-done, f32[32,16,128]{2,1,0:T(8,128)S(1)} %copy-done.1), custom_call_target="tpu_custom_call" | custom-call | tf_op jit(solution)/shard_map/pallas_call | solution.py:270
  94.8 1.1 %copy.7 = f32[5,32,16,128]{3,2,1,0:T(8,128)} copy(f32[5,32,16,128]{3,2,1,0:T(8,128)S(1)} %shard_map.55) | data formatting | bytes 2621440
  (3 shorter events, 0.0 us)
Async XLA Ops:
  1.4 4.8 %collective-permute-start.1 = (f32[11,32]{1,0:T(8,128)S(1)}, f32[11,32]{1,0:T(8,128)S(1)}, u32[]{:S(2)}, u32[]{:S(2)}) collective-permute-start(f32[11,32]{1,0:T(8,128)S(1)} %pad_maximum_fusion), channel_id=1, source_target_pairs={{4,0},{8,4},{12,8},{16,12},{20,16},{24,20},{28,24},{5,1},{9,5},{13... | collective-permute-start | bytes 4232 | tf_op jit(solution)/shard_map/ppermute | solution.py:255
  4.2 5.9 %collective-permute-start = (f32[11,32]{1,0:T(8,128)S(1)}, f32[11,32]{1,0:T(8,128)S(1)}, u32[]{:S(2)}, u32[]{:S(2)}) collective-permute-start(f32[11,32]{1,0:T(8,128)S(1)} %pad_maximum_fusion), channel_id=1, source_target_pairs={{0,4},{4,8},{8,12},{12,16},{16,20},{20,24},{24,28},{1,5},{5,9},{9,... | collective-permute-start | bytes 4232 | tf_op jit(solution)/shard_map/ppermute | solution.py:254
  10.2 1.3 %copy-start = (f32[5,32,16,128]{3,2,1,0:T(8,128)S(1)}, f32[5,32,16,128]{3,2,1,0:T(8,128)}, u32[]{:S(2)}) copy-start(f32[5,32,16,128]{3,2,1,0:T(8,128)} %fields.1) | copy-start | bytes 3932164
  11.5 0.9 copy-start.1

commit v4 on v3

--- a/solution.py
+++ b/solution.py
@@ -29,8 +29,8 @@
     return 2 * column + lax.rem(t, 2), place + odd * (n - 1 - 2 * place)
 
 
-def kernel(n, blocks, srad, sazi, shifts, fields, kappa, out, x0, x1, x2, x3, adv, kap,
-           send1, recv1, send_x, recv_x, send_h, recv_h, send2, recv2):
+def kernel(n, blocks, fast_r, fast_p, shifts, fields, kappa, out, x0, x1, x2, x3, adv, kap,
+           near_r, near_p, near_s, srad, sazi, turns, send_n, recv_n, load_n, send1, recv1, send_x, recv_x, send_h, recv_h, send2, recv2):
     count, rows, width, depth = fields.shape
     own = rows // n
     around = width * n
@@ -59,10 +59,15 @@
     holders = [(home + 1 - 2 * lax.rem(home, 2), jnp.int32(a)) for a in range(n)]
     not_held = [jnp.logical_or(jnp.logical_not(middle), is_me(d)) for d in holders]
 
+    below_in, above_in = rad > 0, rad < blocks // n - 1
+    below = (jnp.maximum(rad - 1, 0), azi)
+    above = (jnp.minimum(rad + 1, blocks // n - 1), azi)
+
     barrier = pltpu.get_barrier_semaphore()
     greeted = jnp.int32(0)
     for device, skip in [*zip(targets, same), *zip(sources, back), (across, across_same),
                          *zip(holders, not_held), (prev, jnp.logical_not(from_prev)),
+                         (below, jnp.logical_not(below_in)), (above, jnp.logical_not(above_in)),
                          (following, jnp.logical_not(from_next))]:
         @pl.when(jnp.logical_not(skip))
         def _():
@@ -130,6 +135,47 @@
             def _():
                 here = x0.at[q, pl.ds(0, HALO)]
                 pltpu.make_async_copy(here, here, recv_x.at[q]).wait()
+
+    small = ((fast_r, near_r, srad), (fast_p, near_p, sazi), (shifts, near_s, turns))
+
+    def speeds(act):
+        for k, (mine_k, near, held_k) in enumerate(small):
+            for side, device, there in ((0, below, below_in), (1, above, above_in)):
+                slot = 1 - side
+                copy = pltpu.make_async_remote_copy(
+                    mine_k, near.at[slot], send_n.at[k, side], recv_n.at[k, slot],
+                    device_id=device, device_id_type=MESH)
+                arrived = pltpu.make_async_remote_copy(
+                    mine_k, near.at[side], send_n.at[k, slot], recv_n.at[k, side],
+                    device_id=device, device_id_type=MESH)
+                inward = pltpu.make_async_copy(
+                    near.at[side], held_k.at[2 * side], load_n.at[k, side])
+
+                @pl.when(there)
+                def _():
+                    if act == "start":
+                        copy.start()
+                    elif act == "send":
+                        copy.wait_send()
+                    elif act == "recv":
+                        arrived.wait_recv()
+                        inward.start()
+                    else:
+                        inward.wait()
+            own_copy = pltpu.make_async_copy(mine_k, held_k.at[1], load_n.at[k, 2])
+            if act == "start":
+                own_copy.start()
+            elif act == "load":
+                own_copy.wait()
+
+    first_row = mine * own - HALO
+    total_rows = blocks * own
+
+    def of_row(table, row, *lead):
+        at = first_row + row
+        inside = jnp.logical_and(at >= 0, at < total_rows)
+        at = jnp.clip(at, 0, total_rows - 1) - (rad - 1) * rows
+        return jnp.where(inside, table[(at // rows, *lead, lax.rem(at, rows))], 0)
 
     lane = lax.broadcasted_iota(jnp.int32, (around, depth), 1)
 
@@ -145,8 +191,10 @@
         one = (r1p + r1m) + (p1p + p1m) + (z1p + z1m)
         two = (r2p + r2m) + (p2p + p2m) + (z2p + z2m)
         spread = 16.0 * one - two - 90.0 * u
-        carried = (srad[f, row] * (8.0 * (r1p - r1m) - (r2p - r2m))
-                   + sazi[f, row] * (8.0 * (p1p - p1m) - (p2p - p2m)))
+        fast = of_row(srad, row, f) * (1.0 / 12.0)
+        slow = of_row(sazi, row, f) * (1.0 / 12.0)
+        carried = (fast * (8.0 * (r1p - r1m) - (r2p - r2m))
+                   + slow * (8.0 * (p1p - p1m) - (p2p - p2m)))
         return u, kap[row] * spread - carried
 
     def each_row(length, value, dst):
@@ -179,9 +227,13 @@
         return carry
 
     first_pass(0, "start")
+    speeds("start")
     lax.fori_loop(1, min(AHEAD, count) + 1, begin, 0)
     lax.fori_loop(0, count + 1, clear, 0)
+    speeds("recv")
     pass_on(0)
+    pass_on(1)
+    speeds("load")
     halo(0, "recv")
 
     each_row(own + 2 * HALO, lambda i: x0[0, i] * (1.0 / 12.0), kap)
@@ -191,42 +243,41 @@
         def _():
             first_pass(t + AHEAD, "start")
 
-        @pl.when(t <= count)
-        def _():
-            pass_on(t)
-
-        @pl.when(t >= 2)
-        def _():
-            q = t - 1
-            f = q - 1
-            halo(q, "recv")
-            base = x0.at[q]
-
-            def value1(i):
-                u, change = operate(base, f, i, i + 2)
-                return u + change
-            each_row(own + 2 * HALO - 4, value1, x1)
-
-            def value2(i):
-                u, change = operate(x1, f, i, i + 4)
-                half = 0.5 * (base[i + 4] + u + change)
-                return pltpu.roll(half, shifts[i + 4], 0)
-            each_row(own + 2 * HALO - 8, value2, x2)
-
-            def value3(i):
-                u, change = operate(x2, f, i, i + 6)
-                return u + change
-            each_row(own + 2 * HALO - 12, value3, x3)
-
-            def value4(i):
-                u, change = operate(x3, f, i, i + 8)
-                return 0.5 * (x2[i + 4] + u + change)
-            each_row(own, value4, adv.at[f])
-            second_pass(f, "start")
+        q = t
+        f = q - 1
+        halo(q, "recv")
+        base = x0.at[q]
+
+        def value1(i):
+            u, change = operate(base, f, i, i + 2)
+            return u + change
+        each_row(own + 2 * HALO - 4, value1, x1)
+
+        def value2(i):
+            u, change = operate(x1, f, i, i + 4)
+            half = 0.5 * (base[i + 4] + u + change)
+            return pltpu.roll(half, of_row(turns, i + 4, 0), 0)
+        each_row(own + 2 * HALO - 8, value2, x2)
+
+        @pl.when(t < count)
+        def _():
+            pass_on(t + 1)
+
+        def value3(i):
+            u, change = operate(x2, f, i, i + 6)
+            return u + change
+        each_row(own + 2 * HALO - 12, value3, x3)
+
+        def value4(i):
+            u, change = operate(x3, f, i, i + 8)
+            return 0.5 * (x2[i + 4] + u + change)
+        each_row(own, value4, adv.at[f])
+        second_pass(f, "start")
         return carry
 
-    lax.fori_loop(1, count + 2, tick, 0)
-
+    lax.fori_loop(1, count + 1, tick, 0)
+
+    speeds("send")
     first_pass(0, "send")
     halo(0, "send")
 
@@ -246,41 +297,33 @@
     own, around = rows // n, width * n
     if own < HALO or n % 2:
         return shards_by_steps(fields, kappa, radial_speed, azimuth_speed, shifts)
-    rad, azi = lax.axis_index("rad"), lax.axis_index("azi")
-    mine = block_of(rad, azi, n)
-    packed = jnp.concatenate(
-        [radial_speed * (1.0 / 12.0), azimuth_speed * (1.0 / 12.0),
-         jnp.mod(shifts, around).astype(jnp.float32)[None]], axis=0)
-    below = lax.ppermute(packed, "rad", [(i, i + 1) for i in range(annuli - 1)])
-    above = lax.ppermute(packed, "rad", [(i + 1, i) for i in range(annuli - 1)])
-    wide = jnp.concatenate([below, packed, above], axis=1)
-    start = mine * own - HALO - (rad - 1) * rows
     tall = own + 2 * HALO
-    wide = lax.dynamic_slice_in_dim(wide, start, tall, axis=1)
-    srad, sazi = wide[:count], wide[count:2 * count]
-    turn = wide[2 * count].astype(jnp.int32)
 
     def scratch(*lead):
         return pltpu.VMEM((*lead, around, depth), jnp.float32)
 
     held = 4 * around * depth * ((count + 2) * tall + 3 * tall + count * own)
     any_space = pl.BlockSpec(memory_space=pl.ANY)
-    small = pl.BlockSpec(memory_space=pltpu.SMEM)
+    table = radial_speed.shape
     dma = pltpu.SemaphoreType.DMA
     return pl.pallas_call(
         functools.partial(kernel, n, n * annuli),
         out_shape=jax.ShapeDtypeStruct(fields.shape, jnp.float32),
-        in_specs=[small, small, small, any_space, any_space],
+        in_specs=[any_space] * 5,
         out_specs=any_space,
         scratch_shapes=[
             scratch(count + 1, tall), scratch(tall - 4), scratch(tall - 8), scratch(tall - 12),
             scratch(count, own), scratch(tall),
+            pltpu.VMEM((2, *table), jnp.float32), pltpu.VMEM((2, *table), jnp.float32),
+            pltpu.VMEM((2, 1, rows), jnp.int32), pltpu.SMEM((3, *table), jnp.float32),
+            pltpu.SMEM((3, *table), jnp.float32), pltpu.SMEM((3, 1, rows), jnp.int32),
+            dma((3, 2)), dma((3, 2)), dma((3, 3)),
             dma((count + 1, n)), dma((count + 1,)), dma((count + 1,)), dma((count + 1,)),
             dma((count + 1, 2)), dma((count + 1, 2)), dma((count, n)), dma((count,)),
         ],
         compiler_params=pltpu.CompilerParams(
             collective_id=0, has_side_effects=True, vmem_limit_bytes=held + (8 << 20)),
-    )(srad, sazi, turn, fields, kappa)
+    )(radial_speed, azimuth_speed, shifts[None], fields, kappa)
 
 
 def kernel_by_steps(n, blocks, srad, sazi, shifts, fields, kappa, out, x0, x1, x2, x3, adv, kap,

time: 96.1 us -> 90.2 us (0.939)
  the two profiles are of different devices: /device:TPU:28 before, /device:TPU:1 now
where the time goes in v4:
time: 90.2 us; the launch traced here: 89.9 us
  Pallas kernels  84.6 us (94%)
  local copies, waits for them, and re-layouts  5.35 us (6%)
    pallas_call x1, Pallas kernels, shards(): pl.pallas_call(functools.partial(kernel, n, n * annuli), out_shape=jax.Sh...  84.6 us
    unnamed x11, local copies, waits for them, and re-layouts  5.35 us

profile of v4, /device:TPU:1, one launch (start us, length us, event | category | flops | bytes accessed | tf_op | source)
XLA Modules:
  0.0 89.9 jit_solution(4852204968234095067)
XLA Ops:
  0.0 0.0 copy-start
  0.0 1.3 %copy-done = f32[5,32,16,128]{3,2,1,0:T(8,128)S(1)} copy-done((f32[5,32,16,128]{3,2,1,0:T(8,128)S(1)}, f32[5,32,16,128]{3,2,1,0:T(8,128)}, u32[]{:S(2)}) %copy-start) | copy-done | bytes 1310744
  1.3 0.0 copy-start.1
  1.3 0.9 %copy-done.1 = f32[32,16,128]{2,1,0:T(8,128)S(1)} copy-done((f32[32,16,128]{2,1,0:T(8,128)S(1)}, f32[32,16,128]{2,1,0:T(8,128)}, u32[]{:S(2)}) %copy-start.1) | copy-done | bytes 262168
  2.3 0.0 copy-start.2
  2.3 0.7 copy-done.2
  3.0 0.0 copy-start.3
  3.0 0.7 copy-done.3
  3.6 0.0 copy-start.4
  3.6 0.7 copy-done.4
  4.3 84.6 %shard_map.55 = f32[5,32,16,128]{3,2,1,0:T(8,128)S(1)} custom-call(f32[5,32]{1,0:T(8,128)S(1)} %copy-done.2, f32[5,32]{1,0:T(8,128)S(1)} %copy-done.3, s32[1,32]{1,0:T(1,128)S(1)} %bitcast.1, f32[5,32,16,128]{3,2,1,0:T(8,128)S(1)} %copy-done, f32[32,16,128]{2,1,0:T(8,128)S(1)} %copy-done.1), custom_call_target="tpu_custom_call" | custom-call | tf_op jit(solution)/shard_map/pallas_call | solution.py:309
  88.9 1.1 %copy.7 = f32[5,32,16,128]{3,2,1,0:T(8,128)} copy(f32[5,32,16,128]{3,2,1,0:T(8,128)S(1)} %shard_map.55) | data formatting | bytes 2621440
Async XLA Ops:
  0.0 1.3 %copy-start = (f32[5,32,16,128]{3,2,1,0:T(8,128)S(1)}, f32[5,32,16,128]{3,2,1,0:T(8,128)}, u32[]{:S(2)}) copy-start(f32[5,32,16,128]{3,2,1,0:T(8,128)} %fields.1) | copy-start | bytes 3932164
  1.3 0.9 %copy-start.1 = (f32[32,16,128]{2,1,0:T(8,128)S(1)}, f32[32,16,128]{2,1,0:T(8,128)}, u32[]{:S(2)}) copy-start(f32[32,16,128]{2,1,0:T(8,128)} %kappa.1) | copy-start | bytes 786436
  2.3 0.7 copy-start.2
  3.0 0.7 copy-start.3
  3.6 0.7 copy-start.4

commit v5 on v4

--- a/solution.py
+++ b/solution.py
@@ -233,16 +233,13 @@
     speeds("recv")
     pass_on(0)
     pass_on(1)
+    lax.fori_loop(min(AHEAD, count) + 1, count + 1, begin, 0)
     speeds("load")
     halo(0, "recv")
 
     each_row(own + 2 * HALO, lambda i: x0[0, i] * (1.0 / 12.0), kap)
 
     def tick(t, carry):
-        @pl.when(t + AHEAD <= count)
-        def _():
-            first_pass(t + AHEAD, "start")
-
         q = t
         f = q - 1
         halo(q, "recv")
@@ -322,7 +319,7 @@
             dma((count + 1, 2)), dma((count + 1, 2)), dma((count, n)), dma((count,)),
         ],
         compiler_params=pltpu.CompilerParams(
-            collective_id=0, has_side_effects=True, vmem_limit_bytes=held + (8 << 20)),
+            collective_id=0, has_side_effects=True, vmem_limit_bytes=max(held + (8 << 20), 60 << 20)),
     )(radial_speed, azimuth_speed, shifts[None], fields, kappa)
 
 

time: 90.2 us -> 90 us (level)
  local copies, waits for them, and re-layouts: 5.35 us -> 2.51 us
  Pallas kernels: 84.6 us -> 86.4 us
    unnamed x11 -> x1, local copies, waits for them, and re-layouts: 5.35 us -> 2.51 us
    pallas_call x1, Pallas kernels: 84.6 us -> 86.4 us  [shards(): pl.pallas_call(functools.partial(kernel, n, n * annuli), out_shape=jax.Sh...]
where the time goes in v5:
time: 90 us; the launch traced here: 88.9 us
  Pallas kernels  86.4 us (96%)
  local copies, waits for them, and re-layouts  2.51 us (3%)
    pallas_call x1, Pallas kernels, shards(): pl.pallas_call(functools.partial(kernel, n, n * annuli), out_shape=jax.Sh...  86.4 us
    unnamed x1, local copies, waits for them, and re-layouts  2.51 us

profile of v5, /device:TPU:1, one launch (start us, length us, event | category | flops | bytes accessed | tf_op | source)
XLA Modules:
  0.0 88.9 jit_solution(3466551170101893021)
XLA Ops:
  0.0 86.4 %shard_map.55 = f32[5,32,16,128]{3,2,1,0:T(8,128)} custom-call(f32[5,32]{1,0:T(8,128)} %fast_r.1, f32[5,32]{1,0:T(8,128)} %fast_p.1, s32[1,32]{1,0:T(1,128)} %bitcast.1, f32[5,32,16,128]{3,2,1,0:T(8,128)} %fields.1, f32[32,16,128]{2,1,0:T(8,128)} %kappa.1), custom_call_target="tpu_custom_call" | custom-call | tf_op jit(solution)/shard_map/pallas_call | solution.py:306
  86.4 2.5 %copy.7 = f32[5,32,16,128]{3,2,1,0:T(8,128)} copy(f32[5,32,16,128]{3,2,1,0:T(8,128)} %shard_map.55) | data formatting | bytes 2621440

commit v6 on v4

--- a/solution.py
+++ b/solution.py
@@ -322,7 +322,7 @@
             dma((count + 1, 2)), dma((count + 1, 2)), dma((count, n)), dma((count,)),
         ],
         compiler_params=pltpu.CompilerParams(
-            collective_id=0, has_side_effects=True, vmem_limit_bytes=held + (8 << 20)),
+            collective_id=0, has_side_effects=True, vmem_limit_bytes=max(held + (8 << 20), 60 << 20)),
     )(radial_speed, azimuth_speed, shifts[None], fields, kappa)
 
 

time: 90.2 us -> 87.6 us (0.971)
  local copies, waits for them, and re-layouts: 5.35 us -> 2.51 us
    unnamed x11 -> x1, local copies, waits for them, and re-layouts: 5.35 us -> 2.51 us
where the time goes in v6:
time: 87.6 us; the launch traced here: 87.4 us
  Pallas kernels  84.9 us (97%)
  local copies, waits for them, and re-layouts  2.51 us (3%)
    pallas_call x1, Pallas kernels, shards(): pl.pallas_call(functools.partial(kernel, n, n * annuli), out_shape=jax.Sh...  84.9 us
    unnamed x1, local copies, waits for them, and re-layouts  2.51 us

profile of v6, /device:TPU:1, one launch (start us, length us, event | category | flops | bytes accessed | tf_op | source)
XLA Modules:
  0.0 87.4 jit_solution(16088002564186329605)
XLA Ops:
  0.0 84.9 %shard_map.55 = f32[5,32,16,128]{3,2,1,0:T(8,128)} custom-call(f32[5,32]{1,0:T(8,128)} %fast_r.1, f32[5,32]{1,0:T(8,128)} %fast_p.1, s32[1,32]{1,0:T(1,128)} %bitcast.1, f32[5,32,16,128]{3,2,1,0:T(8,128)} %fields.1, f32[32,16,128]{2,1,0:T(8,128)} %kappa.1), custom_call_target="tpu_custom_call" | custom-call | tf_op jit(solution)/shard_map/pallas_call | solution.py:309
  84.9 2.5 %copy.7 = f32[5,32,16,128]{3,2,1,0:T(8,128)} copy(f32[5,32,16,128]{3,2,1,0:T(8,128)} %shard_map.55) | data formatting | bytes 2621440
